TPU v7x, 32 devices: a whole 2x2x4 slice. The times are simulated.
32 devices in a mesh: batch: 8 (over z, x), hidden: 4 (over y, core).
Axes of the slice: x: 2, y: 2, z: 4, core: 2. Of those that a mesh axis runs over, the one named last changes fastest.
Arguments:
- tokens: bfloat16 [5120, 4096], P('batch', 'hidden'), may hold values from -18 to 18
- segments: int32 [8, 640], P('batch'), may hold values from 0 to 5, never falling along the last dimension, each value on 1 to 256 neighbouring positions
- rel_bias: float32 [32, 64], P(None, 'hidden'), may hold values from -4 to 4
- ln_gain: float32 [4096], replicated, may hold values from 0.25 to 1.75
- w_query: bfloat16 [4096, 4096], P('batch', 'hidden'), may hold values from -0.04 to 0.04
- w_key: bfloat16 [4096, 4096], P('batch', 'hidden'), may hold values from -1 to 1
- w_value: bfloat16 [4096, 4096], P('batch', 'hidden'), may hold values from -0.09375 to 0.09375
- w_out: bfloat16 [4096, 4096], P('hidden', 'batch'), may hold values from -0.09375 to 0.09375
Outputs:
- output: bfloat16 [5120, 4096], P('batch', 'hidden')
Inputs may be any that keep to these rules, and one draw needn't show every extreme that they name: `segments`: in each row (the 640 tokens of one group) passage ids start at 0 and grow by one at each new passage; every passage has 1 to 256 tokens, one has exactly 256, and all 6 ids occur.
All inputs are finite; a program needn't handle non-finite values.
Results may differ from a plain program's by a relative error of at most 0.0098.
Values may be sent and summed in bfloat16 or wider, within the bound.
No kernel may reach another device: no remote copies, remote signals or barrier semaphores. Data moves between devices by JAX's collectives and lax.ppermute only.
A program may use at most 128 MiB of HBM per device.

v0:
```python
import functools

import jax
import jax.numpy as jnp
from jax import lax
from jax.experimental import pallas as pl
from jax.experimental.pallas import tpu as pltpu
from jax.sharding import PartitionSpec as P

PASSAGE = 256
BLOCK = 128

norm_epsilon = 1e-06
bucket_edges = (12, 16, 23, 32, 46, 64, 91)
masked_score = -1e30


def bucket_of(offsets):
    distance = jnp.abs(offsets)
    reached = sum(((distance >= threshold).astype(jnp.int32) for threshold in bucket_edges))
    within = jnp.where(distance < 8, distance, 8 + reached)
    return within + jnp.where(offsets > 0, 16, 0)


def bias_tiles(table):
    rows = 2 * PASSAGE + BLOCK
    offsets = (
        jnp.arange(rows, dtype=jnp.int32)[:, None]
        - PASSAGE
        - jnp.arange(BLOCK, dtype=jnp.int32)[None, :]
    )
    buckets = bucket_of(offsets)[None]
    tiles = jnp.zeros((table.shape[1], rows, BLOCK), jnp.float32)
    for level in range(table.shape[0]):
        tiles = jnp.where(buckets == level, table[level][:, None, None], tiles)
    return tiles


def attention_kernel(width, q_ids, k_ids, bias, queries, keys, values, out):
    length = keys.shape[0]
    blocks = length // BLOCK
    reach = PASSAGE // BLOCK
    heads = keys.shape[1] // width
    turned = jnp.transpose(values[...].astype(jnp.float32)).astype(jnp.bfloat16)
    head_of = lax.broadcasted_iota(jnp.int32, (BLOCK, keys.shape[1]), 1) // width
    for i in range(blocks):
        low, high = max(0, i - reach) * BLOCK, min(blocks, i + reach + 1) * BLOCK
        columns = slice(i * BLOCK, (i + 1) * BLOCK)
        first = low - i * BLOCK + PASSAGE
        same = k_ids[low:high, :] == q_ids[:, columns]
        own = queries[columns, :]
        results = []
        for h in range(heads):
            chosen = jnp.where(head_of == h, own, jnp.zeros_like(own))
            scores = lax.dot_general(
                keys[low:high, :],
                chosen,
                (((1,), (1,)), ((), ())),
                preferred_element_type=jnp.float32,
            )
            scores = jnp.where(same, scores + bias[h, first : first + high - low, :], masked_score)
            raised = jnp.exp(scores - jnp.max(scores, axis=0, keepdims=True)).astype(jnp.bfloat16)
            extended = jnp.concatenate(
                [
                    turned[h * width : (h + 1) * width, low:high],
                    jnp.ones((16, high - low), jnp.bfloat16),
                ],
                axis=0,
            )
            total = jnp.dot(extended, raised, preferred_element_type=jnp.float32)
            results.append(total[:width] / total[width : width + 1])
        out[columns, :] = jnp.transpose(jnp.concatenate(results, axis=0)).astype(jnp.bfloat16)


def attend(queries, keys, values, ids, bias, width):
    groups, length = ids.shape
    features = keys.shape[1]
    heads = 128 // width
    wide_ids = jnp.broadcast_to(ids.reshape(-1)[:, None], (groups * length, BLOCK))
    block = pl.BlockSpec((length, 128), lambda g, p: (g, p))
    return pl.pallas_call(
        functools.partial(attention_kernel, width),
        grid=(groups, features // 128),
        in_specs=[
            pl.BlockSpec((None, 1, length), lambda g, p: (g, 0, 0)),
            pl.BlockSpec((length, BLOCK), lambda g, p: (g, 0)),
            pl.BlockSpec((heads,) + bias.shape[1:], lambda g, p: (p, 0, 0)),
            block,
            block,
            block,
        ],
        out_specs=block,
        out_shape=jax.ShapeDtypeStruct(queries.shape, jnp.bfloat16),
        compiler_params=pltpu.CompilerParams(vmem_limit_bytes=24 * 1024 * 1024),
        cost_estimate=pl.CostEstimate(
            flops=8 * groups * features * length * length,
            bytes_accessed=16 * groups * features * length,
            transcendentals=groups * features // width * length * length,
        ),
    )(ids[:, None, :], wide_ids, bias, queries, keys, values)


def normalise_kernel(sources, gain, own, peer, out):
    depth = out.shape[1] // sources.shape[0]
    for group, tokens in enumerate((own, peer)):

        @pl.when(pl.program_id(0) == group)
        def _():
            wide = tokens[...].astype(jnp.float32)
            scale = lax.rsqrt(jnp.mean(wide * wide, axis=1, keepdims=True) + norm_epsilon)
            for k in range(sources.shape[0]):
                start = pl.multiple_of(sources[k] * depth, 128)
                part = tokens[:, pl.ds(start, depth)].astype(jnp.float32)
                part = part * scale * gain[:, pl.ds(start, depth)]
                out[:, k * depth : (k + 1) * depth] = part.astype(jnp.bfloat16)


def normalise(own, peer, gain, sources):
    length, size = own.shape
    steps = length // BLOCK
    return pl.pallas_call(
        normalise_kernel,
        grid_spec=pltpu.PrefetchScalarGridSpec(
            num_scalar_prefetch=1,
            grid=(2, steps),
            in_specs=[
                pl.BlockSpec((1, size), lambda g, i, _: (0, 0)),
                pl.BlockSpec((BLOCK, size), lambda g, i, _: (jnp.where(g == 0, i, steps - 1), 0)),
                pl.BlockSpec((BLOCK, size), lambda g, i, _: (jnp.where(g == 0, 0, i), 0)),
            ],
            out_specs=pl.BlockSpec((BLOCK, size), lambda g, i, _: (g * steps + i, 0)),
        ),
        out_shape=jax.ShapeDtypeStruct((2 * length, size), jnp.bfloat16),
        compiler_params=pltpu.CompilerParams(vmem_limit_bytes=24 * 1024 * 1024),
        cost_estimate=pl.CostEstimate(
            flops=16 * length * size, bytes_accessed=8 * length * size, transcendentals=2 * length
        ),
    )(sources, gain[None, :], own, peer)


def after(value, earlier):
    return lax.optimization_barrier((value, earlier))[0]


def per_device(n_batch, n_hidden, tokens, segments, rel_bias, ln_gain, w_query, w_key, w_value, w_out):
    place = lax.axis_index("batch")
    column = lax.axis_index("hidden")
    parity = (place >> 1) & 1
    length, own_width = tokens.shape
    heads = rel_bias.shape[1] // 2
    half = w_query.shape[1] // 2
    width = half // heads

    def swap(value, step, axis="batch"):
        count = n_batch if axis == "batch" else n_hidden
        return lax.ppermute(value, axis, [(i, i ^ step) for i in range(count)])

    far = list(range(4, n_batch, 2))
    far_line, pair_line, near_line = [], [], []

    def paced(value, step, line, depth, *earlier):
        waits = tuple(line[-depth : len(line) - depth + 1]) + earlier
        if waits:
            value = after(value, waits)
        received = swap(value, step)
        line.append(received)
        return received

    def halves(weight, axis):
        size = weight.shape[axis] // 2
        return [
            lax.dynamic_slice_in_dim(weight, side * size, size, axis)
            for side in (parity, 1 - parity)
        ]

    def close_by(parts):
        return jnp.concatenate([parts[0], paced(parts[1], 2, pair_line, 1)], axis=0)

    def far_off(parts):
        distant = {
            step: paced(parts[(step >> 1) & 1], step, far_line, 2) for step in reversed(far)
        }
        return jnp.concatenate([distant[step] for step in far], axis=0)

    def gathered(close):
        planes = n_batch // 4
        size = close.shape[0]
        groups = [[r + 4 * i for i in range(planes)] for r in range(4)]
        whole = lax.all_gather(close, "batch", axis=0, tiled=True, axis_index_groups=groups)
        rest = [
            lax.dynamic_slice_in_dim(whole, ((place >> 2) ^ k) * size, size, 0)
            for k in range(1, planes)
        ]
        return rest[0] if len(rest) == 1 else jnp.concatenate(rest, axis=0)

    def along_x(value, *earlier):
        return paced(value, 1, near_line, 2, *earlier)

    peer_tokens = paced(tokens, 2, pair_line, 1)
    peer_ids = swap(segments, 2)
    own_all, peer_all = [
        lax.all_gather(part, "hidden", axis=1, tiled=True) for part in (tokens, peer_tokens)
    ]

    key_parts, query_parts = halves(w_key, 1), halves(w_query, 1)
    key_close = close_by(key_parts)
    key_far = far_off(key_parts)
    value_close = close_by(halves(w_value, 1))
    query_close = close_by(query_parts)
    query_far = far_off(query_parts)
    out_close = close_by(halves(w_out, 0))

    key_near = along_x(key_close)
    value_near = along_x(value_close)
    value_far = gathered(after(value_close, (own_all, far_line[0])))
    query_near = along_x(query_close)
    key_rest = along_x(key_far)
    query_rest = along_x(query_far)

    order = [0, 2] + far
    order += [step ^ 1 for step in order]
    normed = normalise(own_all, peer_all, ln_gain, jnp.stack([place ^ step for step in order]))

    table = lax.dynamic_slice_in_dim(rel_bias, parity * heads, heads, 1)
    bias = bias_tiles(table)

    def joined(values, axis):
        return values[0] if len(values) == 1 else jnp.concatenate(values, axis=axis)

    def project(*blocks):
        total, first = None, 0
        for rows in blocks:
            part = normed[:, first : first + rows.shape[0]]
            first += rows.shape[0]
            term = jnp.dot(part, rows, preferred_element_type=jnp.float32)
            total = term if total is None else total + term
        return total.astype(jnp.bfloat16)

    keys = project(key_close, key_far, key_near, key_rest)
    queries = project(query_close, query_far, query_near, query_rest)
    out_far = gathered(after(out_close, normed))
    out_near = along_x(out_close, normed)
    value_rest = along_x(value_far, normed)
    values = project(value_close, value_far, value_near, value_rest)
    out_rest = along_x(out_far, values)
    ids = jnp.concatenate([segments, peer_ids], axis=0)
    attended = attend(queries, keys, values, ids, bias, width)

    side = place & 1
    stripes = own_width // (2 * w_out.shape[1])

    def sums(rows):
        def block(step):
            first = (column ^ step) * stripes
            chosen = [
                lax.dynamic_slice_in_dim(rows, ((place >> 1) ^ (first + j)) * half, half, 0)
                for j in range(stripes)
            ]
            chosen = joined(chosen, 1)
            return jnp.dot(attended, chosen, preferred_element_type=jnp.float32)

        far = send(block(3), 1, "hidden")
        near = send(block(1), 1, "hidden")
        return block(0) + near, block(2) + far

    def send(value, step, axis="batch"):
        return swap(value.astype(jnp.bfloat16), step, axis).astype(jnp.float32)

    here, there = sums(jnp.concatenate([out_close, out_far], axis=0))
    received = send(there, 2, "hidden")
    first = here + received
    first = first[:length] + send(first[length:], 2)
    late = after(out_rest, (here, there))
    here, there = sums(jnp.concatenate([out_near, late], axis=0))
    both = send(jnp.concatenate([here[length:], there[length:]], axis=1), 2)
    middle = here.shape[1]
    there = there[:length] + both[:, middle:]
    second = here[:length] + both[:, :middle] + send(there, 2, "hidden")

    parts = [v.reshape(length, stripes, w_out.shape[1]) for v in (first, second)]
    combined = jnp.where(side == 0, jnp.stack(parts, 2), jnp.stack(parts[::-1], 2))
    return (tokens.astype(jnp.float32) + combined.reshape(length, own_width)).astype(jnp.bfloat16)


def solution(mesh):
    placed = (
        P("batch", "hidden"),
        P("batch", None),
        P(None, "hidden"),
        P(),
        P("batch", "hidden"),
        P("batch", "hidden"),
        P("batch", "hidden"),
        P("hidden", "batch"),
    )
    return jax.shard_map(
        functools.partial(per_device, mesh.shape["batch"], mesh.shape["hidden"]),
        mesh=mesh,
        in_specs=placed,
        out_specs=P("batch", "hidden"),
        check_vma=False,
    )
```

profile of v0, /device:TPU:0, one launch (start us, length us, event | category | flops | bytes accessed | tf_op | source)
XLA Modules:
  0.0 391.6 jit_solution(5976794269414590299)
XLA Ops:
  7.3 3.1 collective-permute-start.1
  10.4 29.0 %collective-permute-done.1 = bf16[640,1024]{1,0:T(8,128)(2,1)S(1)} collective-permute-done((bf16[640,1024]{1,0:T(8,128)(2,1)}, bf16[640,1024]{1,0:T(8,128)(2,1)S(1)}, u32[]{:S(2)}, u32[]{:S(2)}) %collective-permute-start.1) | collective-permute-done | bytes 1310752 | tf_op jit(solution)/shard_map/ppermute | solution.py:156
  43.3 11.6 %collective-permute-done.2 = bf16[512,512]{1,0:T(8,128)(2,1)S(1)} collective-permute-done((bf16[512,512]{1,0:T(8,128)(2,1)}, bf16[512,512]{1,0:T(8,128)(2,1)S(1)}, u32[]{:S(2)}, u32[]{:S(2)}) %collective-permute-start.2) | collective-permute-done | bytes 524320 | tf_op jit(solution)/shard_map/ppermute | solution.py:156
  56.3 2.5 collective-permute-start.7
  61.4 9.0 %collective-permute-done.3 = bf16[512,512]{1,0:T(8,128)(2,1)S(1)} collective-permute-done((bf16[512,512]{1,0:T(8,128)(2,1)S(1)}, bf16[512,512]{1,0:T(8,128)(2,1)S(1)}, u32[]{:S(2)}, u32[]{:S(2)}) %collective-permute-start.3) | collective-permute-done | bytes 524320 | tf_op jit(solution)/shard_map/ppermute | solution.py:156
  72.4 2.9 broadcast_compare_fusion.26
  82.1 20.8 %collective-permute-done.5 = bf16[512,512]{1,0:T(8,128)(2,1)} collective-permute-done((bf16[512,512]{1,0:T(8,128)(2,1)S(1)}, bf16[512,512]{1,0:T(8,128)(2,1)}, u32[]{:S(2)}, u32[]{:S(2)}) %collective-permute-start.5) | collective-permute-done | bytes 524320 | tf_op jit(solution)/shard_map/ppermute | solution.py:156
  102.9 3.3 collective-permute-start.6
  113.9 11.8 %select_select_fusion.bias = f32[8,640,128]{2,1,0:T(8,128)} fusion(f32[8]{0:T(128)S(1)} %get-tuple-element.36, f32[8]{0:T(128)S(1)} %get-tuple-element.37, f32[8]{0:T(128)S(1)} %get-tuple-element.38, f32[8]{0:T(128)S(1)} %get-tuple-element.39, f32[8]{0:T(128)S(1)} %get-tuple-element.40, f32[8]{0:T(128)S(1)} %get-tuple-element.41, ...), kind=kLoop, calls=%fused_computation.23 | loop fusion | flops 20971520 | bytes 5243904 | tf_op jit(solution)/shard_map/jit(_where)/select_n | solution.py:35
  125.9 46.1 %collective-permute-done.6 = bf16[512,512]{1,0:T(8,128)(2,1)} collective-permute-done((bf16[512,512]{1,0:T(8,128)(2,1)S(1)}, bf16[512,512]{1,0:T(8,128)(2,1)}, u32[]{:S(2)}, u32[]{:S(2)}) %collective-permute-start.6) | collective-permute-done | bytes 524320 | tf_op jit(solution)/shard_map/ppermute | solution.py:156
  179.3 2.5 copy-done.3
  181.8 2.5 copy-done.4
  184.3 6.4 %shard_map.82 = bf16[1280,4096]{1,0:T(8,128)(2,1)S(1)} custom-call(s32[8]{0:T(128)S(1)} %stack.45.sources, f32[1,4096]{1,0:T(1,128)S(1)} %bitcast.35, bf16[640,4096]{1,0:T(8,128)(2,1)S(1)} %copy-done.3, bf16[640,4096]{1,0:T(8,128)(2,1)S(1)} %copy-done.4), custom_call_target="tpu_custom_call" | custom-call | flops 41943040 | bytes 20971520 | tf_op jit(solution)/shard_map/pallas_call | solution.py:121
  191.3 3.6 fusion.23
  195.4 4.2 %fusion.25 = f32[1280,512]{1,0:T(8,128)} fusion(bf16[1024,512]{1,0:T(8,128)(2,1)} %constant_dynamic-update-slice_fusion, bf16[1280,4096]{1,0:T(8,128)(2,1)S(1)} %shard_map.82), kind=kOutput, calls=%fused_computation.41 | convolution fusion | flops 1342177280 | bytes 6291456 | tf_op jit(solution)/shard_map/dot_general | solution.py:235
  199.7 3.7 fusion.11
  203.4 3.7 fusion.17
  207.1 4.2 %fusion.19 = f32[1280,512]{1,0:T(8,128)} fusion(bf16[1024,512]{1,0:T(8,128)(2,1)} %collective-permute-done.10, bf16[1280,4096]{1,0:T(8,128)(2,1)S(1)} %bitcast.32), kind=kOutput, calls=%fused_computation.35 | convolution fusion | flops 1342177280 | bytes 6291456 | tf_op jit(solution)/shard_map/dot_general | solution.py:235
  211.4 4.4 %fusion.13 = f32[1280,512]{1,0:T(8,128)} fusion(bf16[1024,512]{1,0:T(8,128)(2,1)} %collective-permute-done.11, bf16[1280,4096]{1,0:T(8,128)(2,1)S(1)} %bitcast.32), kind=kOutput, calls=%fused_computation.29 | convolution fusion | flops 1342177280 | bytes 6291456 | tf_op jit(solution)/shard_map/dot_general | solution.py:235
  219.6 6.1 %fusion.6.queries = bf16[1280,512]{1,0:T(8,128)(2,1)S(1)} fusion(f32[1280,512]{1,0:T(8,128)} %fusion.13, f32[1280,512]{1,0:T(8,128)} %fusion.19, f32[1280,512]{1,0:T(8,128)} %fusion.25, bf16[1280,4096]{1,0:T(8,128)(2,1)} %copy-done.2, bf16[512,512]{1,0:T(8,128)(2,1)} %copy-done.18, bf16[512,512]{1,0:T(8,128)(2,1)S(1)} %get-tuple-element.23), kind=kOutput, calls=%fused_computation.13 | convolution fusion | flops 1346895872 | bytes 12845056 | tf_op jit(solution)/shard_map/dot_general | solution.py:235
  225.7 4.1 %fusion.15 = f32[1280,512]{1,0:T(8,128)S(1)} fusion(bf16[1024,512]{1,0:T(8,128)(2,1)} %collective-permute-done.12, bf16[1280,4096]{1,0:T(8,128)(2,1)} %copy-done.2), kind=kOutput, calls=%fused_computation.31 | convolution fusion | flops 1342177280 | bytes 6291456 | tf_op jit(solution)/shard_map/dot_general | solution.py:235
  231.4 11.6 %collective-permute-done.14 = bf16[1024,512]{1,0:T(8,128)(2,1)S(1)} collective-permute-done((bf16[1024,512]{1,0:T(8,128)(2,1)S(1)}, bf16[1024,512]{1,0:T(8,128)(2,1)S(1)}, u32[]{:S(2)}, u32[]{:S(2)}) %collective-permute-start.14) | collective-permute-done | bytes 1048608 | tf_op jit(solution)/shard_map/ppermute | solution.py:156
  246.8 22.5 %shard_map.83 = bf16[1280,512]{1,0:T(8,128)(2,1)S(1)} custom-call(s32[2,1,640]{2,1,0:T(1,128)S(1)} %broadcast_in_dim.413.q_ids, s32[1280,128]{1,0:T(8,128)S(1)} %broadcast_in_dim.415.k_ids, f32[8,640,128]{2,1,0:T(8,128)S(1)} %copy-done.5, bf16[1280,512]{1,0:T(8,128)(2,1)S(1)} %fusion.6.queries, bf16[1280,512]{1,0:T(8,128)(2,1)S(1)} %fusion.7.keys, ...), custom_call_target="tpu_custom_call" | custom-call | flops 3355443200 | bytes 10485760 | tf_op jit(solution)/shard_map/pallas_call | solution.py:81
  269.3 5.0 %all-gather.11.cloned.1.call-done = bf16[2048,512]{1,0:T(8,128)(2,1)} async-done(((bf16[1024,512]{1,0:T(8,128)(2,1)}), bf16[2048,512]{1,0:T(8,128)(2,1)}) %all-gather.11.cloned.1.call-update) | async-done | bytes 2097168 | tf_op jit(solution)/shard_map/all_gather | solution.py:189
  280.1 3.0 convolution_convert_fusion.3
  288.7 2.4 convolution_add_fusion.3
  291.2 17.5 %collective-permute-done.21 = bf16[1024,512]{1,0:T(8,128)(2,1)S(1)} collective-permute-done((bf16[1024,512]{1,0:T(8,128)(2,1)S(1)}, bf16[1024,512]{1,0:T(8,128)(2,1)S(1)}, u32[]{:S(2)}, u32[]{:S(2)}) %collective-permute-start.21) | collective-permute-done | bytes 1048608 | tf_op jit(solution)/shard_map/ppermute | solution.py:156
  315.7 16.3 %collective-permute-start.24 = (bf16[640,1024]{0,1:T(8,128)(2,1)S(1)}, bf16[640,1024]{0,1:T(8,128)(2,1)S(1)}, u32[]{:S(2)}, u32[]{:S(2)}) collective-permute-start(bf16[640,1024]{0,1:T(8,128)(2,1)S(1)} %pad_maximum_fusion.1), channel_id=1, source_target_pairs={{0,8},{4,12},{8,0},{12,4},{16,24},{20,28},{24,16},{28,20},{1,9},{5... | collective-permute-start | bytes 3932168 | tf_op jit(solution)/shard_map/ppermute | solution.py:156
  332.0 9.9 %collective-permute-done.18 = bf16[1280,512]{0,1:T(8,128)(2,1)S(1)} collective-permute-done((bf16[1280,512]{0,1:T(8,128)(2,1)S(1)}, bf16[1280,512]{0,1:T(8,128)(2,1)S(1)}, u32[]{:S(2)}, u32[]{:S(2)}) %collective-permute-start.18) | collective-permute-done | bytes 1310752 | tf_op jit(solution)/shard_map/ppermute | solution.py:156
  343.2 16.2 %collective-permute-start.19 = (bf16[640,512]{0,1:T(8,128)(2,1)}, bf16[640,512]{0,1:T(8,128)(2,1)}, u32[]{:S(2)}, u32[]{:S(2)}) collective-permute-start(bf16[640,512]{0,1:T(8,128)(2,1)} %slice.273), channel_id=1, source_target_pairs={{0,8},{4,12},{8,0},{12,4},{16,24},{20,28},{24,16},{28,20},{1,9},{5... | collective-permute-start | bytes 1966088 | tf_op jit(solution)/shard_map/ppermute | solution.py:156
  364.3 10.9 %collective-permute-done.19 = bf16[640,512]{0,1:T(8,128)(2,1)} collective-permute-done((bf16[640,512]{0,1:T(8,128)(2,1)}, bf16[640,512]{0,1:T(8,128)(2,1)}, u32[]{:S(2)}, u32[]{:S(2)}) %collective-permute-start.19) | collective-permute-done | bytes 655392 | tf_op jit(solution)/shard_map/ppermute | solution.py:156
  381.3 3.6 add_convert_fusion
  (160 shorter events, 73.3 us)
Async XLA Ops:
  6.5 68.8 %copy-start = (f32[32,16]{0,1:T(8,128)S(1)}, f32[32,16]{0,1:T(8,128)}, u32[]{:S(2)}) copy-start(f32[32,16]{0,1:T(8,128)} %param.10) | copy-start | bytes 6148
  6.5 106.5 %all-gather.5.cloned.1.call-start = ((), (), s32[]{:S(2)}) async-start(), calls=%async_computation | async-start | bytes 6553600 | tf_op jit(solution)/shard_map/all_gather | solution.py:202
  7.3 172.1 %all-gather.7.cloned.1.call-start = ((), (), s32[]{:S(2)}) async-start(), calls=%async_computation.1 | async-start | bytes 6553600 | tf_op jit(solution)/shard_map/all_gather | solution.py:202
  7.3 32.1 %collective-permute-start.1 = (bf16[640,1024]{1,0:T(8,128)(2,1)}, bf16[640,1024]{1,0:T(8,128)(2,1)S(1)}, u32[]{:S(2)}, u32[]{:S(2)}) collective-permute-start(bf16[640,1024]{1,0:T(8,128)(2,1)} %param.8), channel_id=1, source_target_pairs={{0,8},{4,12},{8,0},{12,4},{16,24},{20,28},{24,16},{28,20},{1,9},{5... | collective-permute-start | bytes 3932168 | tf_op jit(solution)/shard_map/ppermute | solution.py:156
  40.5 177.1 %all-gather.9.cloned.1.call-start = ((), (), s32[]{:S(2)}) async-start(), calls=%async_computation.2 | async-start | bytes 3145728 | tf_op jit(solution)/shard_map/all_gather | solution.py:189
  41.4 13.4 %collective-permute-start.2 = (bf16[512,512]{1,0:T(8,128)(2,1)}, bf16[512,512]{1,0:T(8,128)(2,1)S(1)}, u32[]{:S(2)}, u32[]{:S(2)}) collective-permute-start(bf16[512,512]{1,0:T(8,128)(2,1)} %get-tuple-element.20), channel_id=1, source_target_pairs={{0,8},{4,12},{8,0},{12,4},{16,24},{20,28},{24,16},{28,20},{1,9},{5... | collective-permute-start | bytes 1572872 | tf_op jit(solution)/shard_map/ppermute | solution.py:156
  54.9 15.6 %collective-permute-start.3 = (bf16[512,512]{1,0:T(8,128)(2,1)S(1)}, bf16[512,512]{1,0:T(8,128)(2,1)S(1)}, u32[]{:S(2)}, u32[]{:S(2)}) collective-permute-start(bf16[512,512]{1,0:T(8,128)(2,1)S(1)} %get-tuple-element.21), channel_id=1, source_target_pairs={{0,8},{4,12},{8,0},{12,4},{16,24},{20,28},{24,16},{28,20},{1,9},{5... | collective-permute-start | bytes 1572872 | tf_op jit(solution)/shard_map/ppermute | solution.py:156
  56.3 46.6 %collective-permute-start.7 = (bf16[512,512]{1,0:T(8,128)(2,1)}, bf16[512,512]{1,0:T(8,128)(2,1)}, u32[]{:S(2)}, u32[]{:S(2)}) collective-permute-start(bf16[512,512]{1,0:T(8,128)(2,1)} %get-tuple-element.20), channel_id=1, source_target_pairs={{0,24},{4,28},{8,16},{12,20},{16,8},{20,12},{24,0},{28,4},{1,25},{... | collective-permute-start | bytes 1572872 | tf_op jit(solution)/shard_map/ppermute | solution.py:156
  58.8 44.1 %collective-permute-start.5 = (bf16[512,512]{1,0:T(8,128)(2,1)S(1)}, bf16[512,512]{1,0:T(8,128)(2,1)}, u32[]{:S(2)}, u32[]{:S(2)}) collective-permute-start(bf16[512,512]{1,0:T(8,128)(2,1)S(1)} %get-tuple-element.72), channel_id=1, source_target_pairs={{0,16},{4,20},{8,24},{12,28},{16,0},{20,4},{24,8},{28,12},{1,17},{... | collective-permute-start | bytes 1572872 | tf_op jit(solution)/shard_map/ppermute | solution.py:156
  60.0 51.6 %collective-permute-start.9 = (bf16[1024,512]{1,0:T(8,128)(2,1)}, bf16[1024,512]{1,0:T(8,128)(2,1)}, u32[]{:S(2)}, u32[]{:S(2)}) collective-permute-start(bf16[1024,512]{1,0:T(8,128)(2,1)} %pad_maximum_fusion.3), channel_id=1, source_target_pairs={{0,4},{4,0},{8,12},{12,8},{16,20},{20,16},{24,28},{28,24},{1,5},{5... | collective-permute-start | bytes 3145736 | tf_op jit(solution)/shard_map/ppermute | solution.py:156
  72.4 40.7 %collective-permute-start.12 = (bf16[1024,512]{1,0:T(8,128)(2,1)}, bf16[1024,512]{1,0:T(8,128)(2,1)}, u32[]{:S(2)}, u32[]{:S(2)}) collective-permute-start(bf16[1024,512]{1,0:T(8,128)(2,1)} %pad_maximum_fusion.4), channel_id=1, source_target_pairs={{0,4},{4,0},{8,12},{12,8},{16,20},{20,16},{24,28},{28,24},{1,5},{5... | collective-permute-start | bytes 3145736 | tf_op jit(solution)/shard_map/ppermute | solution.py:156
  76.3 32.0 %collective-permute-start.4 = (bf16[512,512]{1,0:T(8,128)(2,1)}, bf16[512,512]{1,0:T(8,128)(2,1)S(1)}, u32[]{:S(2)}, u32[]{:S(2)}) collective-permute-start(bf16[512,512]{1,0:T(8,128)(2,1)} %get-tuple-element.22), channel_id=1, source_target_pairs={{0,8},{4,12},{8,0},{12,4},{16,24},{20,28},{24,16},{28,20},{1,9},{5... | collective-permute-start | bytes 1572872 | tf_op jit(solution)/shard_map/ppermute | solution.py:156
  82.1 93.7 %copy-start.10 = (bf16[512,512]{1,0:T(8,128)(2,1)}, bf16[512,512]{1,0:T(8,128)(2,1)S(1)}, u32[]{:S(2)}) copy-start(bf16[512,512]{1,0:T(8,128)(2,1)S(1)} %get-tuple-element.67) | copy-start | bytes 1572868
  102.8 10.4 %collective-permute-start = (s32[1,640]{1,0:T(1,128)S(1)}, s32[1,640]{1,0:T(1,128)S(1)}, u32[]{:S(2)}, u32[]{:S(2)}) collective-permute-start(s32[1,640]{1,0:T(1,128)S(1)} %copy-done.25), channel_id=1, source_target_pairs={{0,8},{4,12},{8,0},{12,4},{16,24},{20,28},{24,16},{28,20},{1,9},{5... | collective-permute-start | bytes 7688 | tf_op jit(solution)/shard_map/ppermute | solution.py:156
  102.9 69.1 %collective-permute-start.6 = (bf16[512,512]{1,0:T(8,128)(2,1)S(1)}, bf16[512,512]{1,0:T(8,128)(2,1)}, u32[]{:S(2)}, u32[]{:S(2)}) collective-permute-start(bf16[512,512]{1,0:T(8,128)(2,1)S(1)} %get-tuple-element.23), channel_id=1, source_target_pairs={{0,16},{4,20},{8,24},{12,28},{16,0},{20,4},{24,8},{28,12},{1,17},{... | collective-permute-start | bytes 1572872 | tf_op jit(solution)/shard_map/ppermute | solution.py:156
  109.3 64.5 %collective-permute-start.8 = (bf16[512,512]{1,0:T(8,128)(2,1)}, bf16[512,512]{1,0:T(8,128)(2,1)}, u32[]{:S(2)}, u32[]{:S(2)}) collective-permute-start(bf16[512,512]{1,0:T(8,128)(2,1)} %get-tuple-element.22), channel_id=1, source_target_pairs={{0,24},{4,28},{8,16},{12,20},{16,8},{20,12},{24,0},{28,4},{1,25},{... | collective-permute-start | bytes 1572872 | tf_op jit(solution)/shard_map/ppermute | solution.py:156
  111.5 66.3 %collective-permute-start.10 = (bf16[1024,512]{1,0:T(8,128)(2,1)}, bf16[1024,512]{1,0:T(8,128)(2,1)}, u32[]{:S(2)}, u32[]{:S(2)}) collective-permute-start(bf16[1024,512]{1,0:T(8,128)(2,1)} %pad_maximum_fusion.2), channel_id=1, source_target_pairs={{0,4},{4,0},{8,12},{12,8},{16,20},{20,16},{24,28},{28,24},{1,5},{5... | collective-permute-start | bytes 3145736 | tf_op jit(solution)/shard_map/ppermute | solution.py:156
  113.0 62.7 %collective-permute-start.15 = (bf16[512,512]{1,0:T(8,128)(2,1)}, bf16[512,512]{1,0:T(8,128)(2,1)}, u32[]{:S(2)}, u32[]{:S(2)}) collective-permute-start(bf16[512,512]{1,0:T(8,128)(2,1)} %get-tuple-element.30), channel_id=1, source_target_pairs={{0,8},{4,12},{8,0},{12,4},{16,24},{20,28},{24,16},{28,20},{1,9},{5... | collective-permute-start | bytes 1572872 | tf_op jit(solution)/shard_map/ppermute | solution.py:156
  113.0 161.2 %all-gather.11.cloned.1.call-start = ((), (), s32[]{:S(2)}) async-start(), calls=%async_computation.3 | async-start | bytes 3145728 | tf_op jit(solution)/shard_map/all_gather | solution.py:189
  113.3 77.4 %collective-permute-start.13 = (bf16[1024,512]{1,0:T(8,128)(2,1)}, bf16[1024,512]{1,0:T(8,128)(2,1)}, u32[]{:S(2)}, u32[]{:S(2)}) collective-permute-start(bf16[1024,512]{1,0:T(8,128)(2,1)} %copy-done.23), channel_id=1, source_target_pairs={{0,4},{4,0},{8,12},{12,8},{16,20},{20,16},{24,28},{28,24},{1,5},{5... | collective-permute-start | bytes 3145736 | tf_op jit(solution)/shard_map/ppermute | solution.py:156
  177.8 33.6 %collective-permute-start.11 = (bf16[1024,512]{1,0:T(8,128)(2,1)}, bf16[1024,512]{1,0:T(8,128)(2,1)}, u32[]{:S(2)}, u32[]{:S(2)}) collective-permute-start(bf16[1024,512]{1,0:T(8,128)(2,1)} %constant_dynamic-update-slice_fusion), channel_id=1, source_target_pairs={{0,4},{4,0},{8,12},{12,8},{16,20},{20,16},{24,28},{28,24},{1,5},{5... | collective-permute-start | bytes 3145736 | tf_op jit(solution)/shard_map/ppermute | solution.py:156
  190.7 92.9 %collective-permute-start.20 = (bf16[1024,512]{1,0:T(8,128)(2,1)}, bf16[1024,512]{1,0:T(8,128)(2,1)}, u32[]{:S(2)}, u32[]{:S(2)}) collective-permute-start(bf16[1024,512]{1,0:T(8,128)(2,1)} %pad_maximum_fusion.5), channel_id=1, source_target_pairs={{0,4},{4,0},{8,12},{12,8},{16,20},{20,16},{24,28},{28,24},{1,5},{5... | collective-permute-start | bytes 3145736 | tf_op jit(solution)/shard_map/ppermute | solution.py:156
  218.9 24.1 %collective-permute-start.14 = (bf16[1024,512]{1,0:T(8,128)(2,1)S(1)}, bf16[1024,512]{1,0:T(8,128)(2,1)S(1)}, u32[]{:S(2)}, u32[]{:S(2)}) collective-permute-start(bf16[1024,512]{1,0:T(8,128)(2,1)S(1)} %constant_dynamic-slice_fusion.3), channel_id=1, source_target_pairs={{0,4},{4,0},{8,12},{12,8},{16,20},{20,16},{24,28},{28,24},{1,5},{5... | collective-permute-start | bytes 3145736 | tf_op jit(solution)/shard_map/ppermute | solution.py:156
  280.1 6.3 %collective-permute-start.17 = (bf16[1280,512]{0,1:T(8,128)(2,1)}, bf16[1280,512]{0,1:T(8,128)(2,1)}, u32[]{:S(2)}, u32[]{:S(2)}) collective-permute-start(bf16[1280,512]{0,1:T(8,128)(2,1)} %convolution_convert_fusion.2), channel_id=1, source_target_pairs={{0,1},{1,0},{2,3},{3,2},{4,5},{5,4},{6,7},{7,6},{8,9},{9,8},{10,11... | collective-permute-start | bytes 3932168 | tf_op jit(solution)/shard_map/ppermute | solution.py:156
  283.1 5.7 %collective-permute-start.16 = (bf16[1280,512]{0,1:T(8,128)(2,1)}, bf16[1280,512]{0,1:T(8,128)(2,1)}, u32[]{:S(2)}, u32[]{:S(2)}) collective-permute-start(bf16[1280,512]{0,1:T(8,128)(2,1)} %convolution_convert_fusion.3), channel_id=1, source_target_pairs={{0,1},{1,0},{2,3},{3,2},{4,5},{5,4},{6,7},{7,6},{8,9},{9,8},{10,11... | collective-permute-start | bytes 3932168 | tf_op jit(solution)/shard_map/ppermute | solution.py:156
  283.6 25.1 %collective-permute-start.21 = (bf16[1024,512]{1,0:T(8,128)(2,1)S(1)}, bf16[1024,512]{1,0:T(8,128)(2,1)S(1)}, u32[]{:S(2)}, u32[]{:S(2)}) collective-permute-start(bf16[1024,512]{1,0:T(8,128)(2,1)S(1)} %constant_dynamic-slice_fusion), channel_id=1, source_target_pairs={{0,4},{4,0},{8,12},{12,8},{16,20},{20,16},{24,28},{28,24},{1,5},{5... | collective-permute-start | bytes 3145736 | tf_op jit(solution)/shard_map/ppermute | solution.py:156
  309.6 3.1 collective-permute-start.22
  310.6 4.0 %collective-permute-start.23 = (bf16[1280,512]{0,1:T(8,128)(2,1)S(1)}, bf16[1280,512]{0,1:T(8,128)(2,1)S(1)}, u32[]{:S(2)}, u32[]{:S(2)}) collective-permute-start(bf16[1280,512]{0,1:T(8,128)(2,1)S(1)} %convolution_convert_fusion), channel_id=1, source_target_pairs={{0,1},{1,0},{2,3},{3,2},{4,5},{5,4},{6,7},{7,6},{8,9},{9,8},{10,11... | collective-permute-start | bytes 3932168 | tf_op jit(solution)/shard_map/ppermute | solution.py:156
  311.2 30.8 %collective-permute-start.18 = (bf16[1280,512]{0,1:T(8,128)(2,1)S(1)}, bf16[1280,512]{0,1:T(8,128)(2,1)S(1)}, u32[]{:S(2)}, u32[]{:S(2)}) collective-permute-start(bf16[1280,512]{0,1:T(8,128)(2,1)S(1)} %convolution_add_fusion.2), channel_id=1, source_target_pairs={{0,2},{1,3},{2,0},{3,1},{4,6},{5,7},{6,4},{7,5},{8,10},{9,11},{10,... | collective-permute-start | bytes 3932168 | tf_op jit(solution)/shard_map/ppermute | solution.py:156
  315.7 45.8 %collective-permute-start.24 = (bf16[640,1024]{0,1:T(8,128)(2,1)S(1)}, bf16[640,1024]{0,1:T(8,128)(2,1)S(1)}, u32[]{:S(2)}, u32[]{:S(2)}) collective-permute-start(bf16[640,1024]{0,1:T(8,128)(2,1)S(1)} %pad_maximum_fusion.1), channel_id=1, source_target_pairs={{0,8},{4,12},{8,0},{12,4},{16,24},{20,28},{24,16},{28,20},{1,9},{5... | collective-permute-start | bytes 3932168 | tf_op jit(solution)/shard_map/ppermute | solution.py:156
  343.2 32.0 %collective-permute-start.19 = (bf16[640,512]{0,1:T(8,128)(2,1)}, bf16[640,512]{0,1:T(8,128)(2,1)}, u32[]{:S(2)}, u32[]{:S(2)}) collective-permute-start(bf16[640,512]{0,1:T(8,128)(2,1)} %slice.273), channel_id=1, source_target_pairs={{0,8},{4,12},{8,0},{12,4},{16,24},{20,28},{24,16},{28,20},{1,9},{5... | collective-permute-start | bytes 1966088 | tf_op jit(solution)/shard_map/ppermute | solution.py:156
  362.8 16.0 %collective-permute-start.25 = (bf16[640,512]{0,1:T(8,128)(2,1)}, bf16[640,512]{0,1:T(8,128)(2,1)S(1)}, u32[]{:S(2)}, u32[]{:S(2)}) collective-permute-start(bf16[640,512]{0,1:T(8,128)(2,1)} %fusion.30), channel_id=1, source_target_pairs={{0,2},{1,3},{2,0},{3,1},{4,6},{5,7},{6,4},{7,5},{8,10},{9,11},{10,... | collective-permute-start | bytes 1966088 | tf_op jit(solution)/shard_map/ppermute | solution.py:156
  (30 other events, 359.3 us)
Sparse Core Ops, SparseCore 0:
  8.9 43.1 all-gather.4
  53.7 40.4 all-gather.6
  113.2 80.6 all-gather.8
  199.8 74.4 all-gather.10
where the time goes:
time: 396 us; the launch traced here: 392 us
  waiting for transfers between devices  177 us (45%)
  starting transfers between devices  60.1 us (15%)
  matrix products  54.3 us (14%)
  local copies, waits for them, and re-layouts  28.8 us (7%)
  Pallas kernels  28.8 us (7%)
  other arithmetic  28.5 us (7%)
  between operations  13.9 us (4%)
    ppermute x26, waiting for transfers between devices, swap(): return lax.ppermute(value, axis, [(i, i ^ step) for i in range(count)])  171 us
    ppermute x26, starting transfers between devices, swap(): return lax.ppermute(value, axis, [(i, i ^ step) for i in range(count)])  59.8 us
    dot_general x12, matrix products, project(): term = jnp.dot(part, rows, preferred_element_type=jnp.float32)  40.9 us
    pallas_call x1, Pallas kernels, attend(): pl.pallas_call(functools.partial(attention_kernel, width), grid=(groups,...  22.5 us
    unnamed x67, local copies, waits for them, and re-layouts  14 us
    dot_general x8, matrix products, block(): return jnp.dot(attended, chosen, preferred_element_type=jnp.float32)  13.4 us
    select_n x1, other arithmetic, bias_tiles(): tiles = jnp.where(buckets == level, table[level][:, None, None], tiles)  11.8 us
  transfers between devices with their start and end apart: 30, of which 14 were waited for; matrix products, arithmetic and copies ran while one was open for 24% of the time, Pallas kernels for 7%

commit v1 on v0

--- a/solution.py
+++ b/solution.py
@@ -196,23 +196,24 @@
     def along_x(value, *earlier):
         return paced(value, 1, near_line, 2, *earlier)
 
-    peer_tokens = paced(tokens, 2, pair_line, 1)
+    key_parts, query_parts = halves(w_key, 1), halves(w_query, 1)
+    value_close = close_by(halves(w_value, 1))
+    key_far = far_off(key_parts)
+
+    peer_tokens = paced(tokens, 2, pair_line, 1, far_line[0])
     peer_ids = swap(segments, 2)
     own_all, peer_all = [
         lax.all_gather(part, "hidden", axis=1, tiled=True) for part in (tokens, peer_tokens)
     ]
 
-    key_parts, query_parts = halves(w_key, 1), halves(w_query, 1)
     key_close = close_by(key_parts)
-    key_far = far_off(key_parts)
-    value_close = close_by(halves(w_value, 1))
     query_close = close_by(query_parts)
     query_far = far_off(query_parts)
     out_close = close_by(halves(w_out, 0))
 
+    value_near = along_x(value_close)
     key_near = along_x(key_close)
-    value_near = along_x(value_close)
-    value_far = gathered(after(value_close, (own_all, far_line[0])))
+    value_far = gathered(after(value_close, own_all))
     query_near = along_x(query_close)
     key_rest = along_x(key_far)
     query_rest = along_x(query_far)

time: 396 us -> 390 us (0.985)
  waiting for transfers between devices: 177 us -> 173 us
    ppermute x26, waiting for transfers between devices: 171 us -> 162 us  [swap(): return lax.ppermute(value, axis, [(i, i ^ step) for i in range(count)])]
    all_gather x2, waiting for transfers between devices: 5.01 us -> 9.93 us  [gathered(): lax.all_gather(close, 'batch', axis=0, tiled=True, axis_index_groups=groups)]
    unnamed x67 -> x93, local copies, waits for them, and re-layouts: 14 us -> 10.9 us
  transfers between devices with their start and end apart: 30 -> 30, of which waited for: 14 -> 15; matrix products, arithmetic and copies ran while one was open for 24% -> 24% of each run, Pallas kernels for 7% -> 7%
where the time goes in v1:
time: 390 us; the launch traced here: 386 us
  waiting for transfers between devices  173 us (44%)
  starting transfers between devices  63.2 us (16%)
  matrix products  53.2 us (14%)
  Pallas kernels  28.8 us (7%)
  other arithmetic  28 us (7%)
  local copies, waits for them, and re-layouts  25.4 us (7%)
  between operations  14.1 us (4%)
    ppermute x26, waiting for transfers between devices, swap(): return lax.ppermute(value, axis, [(i, i ^ step) for i in range(count)])  162 us
    ppermute x26, starting transfers between devices, swap(): return lax.ppermute(value, axis, [(i, i ^ step) for i in range(count)])  62.9 us
    dot_general x12, matrix products, project(): term = jnp.dot(part, rows, preferred_element_type=jnp.float32)  39.8 us
    pallas_call x1, Pallas kernels, attend(): pl.pallas_call(functools.partial(attention_kernel, width), grid=(groups,...  22.5 us
    dot_general x8, matrix products, block(): return jnp.dot(attended, chosen, preferred_element_type=jnp.float32)  13.4 us
    select_n x1, other arithmetic, bias_tiles(): tiles = jnp.where(buckets == level, table[level][:, None, None], tiles)  12.1 us
    unnamed x93, local copies, waits for them, and re-layouts  10.9 us
    all_gather x2, waiting for transfers between devices, gathered(): lax.all_gather(close, 'batch', axis=0, tiled=True, axis_index_groups=groups)  9.93 us
  transfers between devices with their start and end apart: 30, of which 15 were waited for; matrix products, arithmetic and copies ran while one was open for 24% of the time, Pallas kernels for 7%

profile of v1, /device:TPU:0, one launch (start us, length us, event | category | flops | bytes accessed | tf_op | source)
XLA Modules:
  0.0 385.7 jit_solution(3103236566268054753)
XLA Ops:
  8.7 5.1 %collective-permute-start.2 = (bf16[512,512]{1,0:T(8,128)(2,1)S(1)}, bf16[512,512]{1,0:T(8,128)(2,1)S(1)}, u32[]{:S(2)}, u32[]{:S(2)}) collective-permute-start(bf16[512,512]{1,0:T(8,128)(2,1)S(1)} %get-tuple-element.21), channel_id=1, source_target_pairs={{0,24},{4,28},{8,16},{12,20},{16,8},{20,12},{24,0},{28,4},{1,25},{... | collective-permute-start | bytes 1572872 | tf_op jit(solution)/shard_map/ppermute | solution.py:156
  14.0 12.7 %collective-permute-done.2 = bf16[512,512]{1,0:T(8,128)(2,1)S(1)} collective-permute-done((bf16[512,512]{1,0:T(8,128)(2,1)S(1)}, bf16[512,512]{1,0:T(8,128)(2,1)S(1)}, u32[]{:S(2)}, u32[]{:S(2)}) %collective-permute-start.2) | collective-permute-done | bytes 524320 | tf_op jit(solution)/shard_map/ppermute | solution.py:156
  26.7 10.4 %collective-permute-done.1 = bf16[512,512]{1,0:T(8,128)(2,1)S(1)} collective-permute-done((bf16[512,512]{1,0:T(8,128)(2,1)S(1)}, bf16[512,512]{1,0:T(8,128)(2,1)S(1)}, u32[]{:S(2)}, u32[]{:S(2)}) %collective-permute-start.1) | collective-permute-done | bytes 524320 | tf_op jit(solution)/shard_map/ppermute | solution.py:156
  38.8 29.2 %collective-permute-done.3 = bf16[640,1024]{1,0:T(8,128)(2,1)} collective-permute-done((bf16[640,1024]{1,0:T(8,128)(2,1)S(1)}, bf16[640,1024]{1,0:T(8,128)(2,1)}, u32[]{:S(2)}, u32[]{:S(2)}) %collective-permute-start.3) | collective-permute-done | bytes 1310752 | tf_op jit(solution)/shard_map/ppermute | solution.py:156
  72.8 17.5 %collective-permute-done.4 = bf16[512,512]{1,0:T(8,128)(2,1)S(1)} collective-permute-done((bf16[512,512]{1,0:T(8,128)(2,1)}, bf16[512,512]{1,0:T(8,128)(2,1)S(1)}, u32[]{:S(2)}, u32[]{:S(2)}) %collective-permute-start.4) | collective-permute-done | bytes 524320 | tf_op jit(solution)/shard_map/ppermute | solution.py:156
  92.6 3.1 broadcast_compare_fusion.26
  101.5 2.7 collective-permute-start.7
  105.4 10.8 %collective-permute-done.5 = bf16[512,512]{1,0:T(8,128)(2,1)S(1)} collective-permute-done((bf16[512,512]{1,0:T(8,128)(2,1)}, bf16[512,512]{1,0:T(8,128)(2,1)S(1)}, u32[]{:S(2)}, u32[]{:S(2)}) %collective-permute-start.5) | collective-permute-done | bytes 524320 | tf_op jit(solution)/shard_map/ppermute | solution.py:156
  122.0 12.1 %select_select_fusion.bias = f32[8,640,128]{2,1,0:T(8,128)} fusion(f32[8]{0:T(128)S(1)} %get-tuple-element.36, f32[8]{0:T(128)S(1)} %get-tuple-element.37, f32[8]{0:T(128)S(1)} %get-tuple-element.38, f32[8]{0:T(128)S(1)} %get-tuple-element.39, f32[8]{0:T(128)S(1)} %get-tuple-element.40, f32[8]{0:T(128)S(1)} %get-tuple-element.41, ...), kind=kLoop, calls=%fused_computation.23 | loop fusion | flops 20971520 | bytes 5243904 | tf_op jit(solution)/shard_map/jit(_where)/select_n | solution.py:35
  134.3 33.9 %collective-permute-done.7 = bf16[512,512]{1,0:T(8,128)(2,1)} collective-permute-done((bf16[512,512]{1,0:T(8,128)(2,1)S(1)}, bf16[512,512]{1,0:T(8,128)(2,1)}, u32[]{:S(2)}, u32[]{:S(2)}) %collective-permute-start.7) | collective-permute-done | bytes 524320 | tf_op jit(solution)/shard_map/ppermute | solution.py:156
  173.5 2.5 copy-done.3
  176.0 2.5 copy-done.4
  178.5 6.4 %shard_map.82 = bf16[1280,4096]{1,0:T(8,128)(2,1)S(1)} custom-call(s32[8]{0:T(128)S(1)} %stack.45.sources, f32[1,4096]{1,0:T(1,128)S(1)} %bitcast.35, bf16[640,4096]{1,0:T(8,128)(2,1)S(1)} %copy-done.3, bf16[640,4096]{1,0:T(8,128)(2,1)S(1)} %copy-done.4), custom_call_target="tpu_custom_call" | custom-call | flops 41943040 | bytes 20971520 | tf_op jit(solution)/shard_map/pallas_call | solution.py:121
  186.0 3.7 fusion.23
  189.7 3.0 fusion.25
  192.8 3.7 fusion.11
  196.5 3.7 fusion.17
  200.2 4.3 %fusion.19 = f32[1280,512]{1,0:T(8,128)} fusion(bf16[1024,512]{1,0:T(8,128)(2,1)} %collective-permute-done.10, bf16[1280,4096]{1,0:T(8,128)(2,1)S(1)} %bitcast.32), kind=kOutput, calls=%fused_computation.35 | convolution fusion | flops 1342177280 | bytes 6291456 | tf_op jit(solution)/shard_map/dot_general | solution.py:236
  204.5 4.4 %fusion.13 = f32[1280,512]{1,0:T(8,128)} fusion(bf16[1024,512]{1,0:T(8,128)(2,1)} %collective-permute-done.11, bf16[1280,4096]{1,0:T(8,128)(2,1)S(1)} %bitcast.32), kind=kOutput, calls=%fused_computation.29 | convolution fusion | flops 1342177280 | bytes 6291456 | tf_op jit(solution)/shard_map/dot_general | solution.py:236
  213.1 6.4 %fusion.6.queries = bf16[1280,512]{1,0:T(8,128)(2,1)S(1)} fusion(f32[1280,512]{1,0:T(8,128)} %fusion.13, f32[1280,512]{1,0:T(8,128)} %fusion.19, f32[1280,512]{1,0:T(8,128)} %fusion.25, bf16[1280,4096]{1,0:T(8,128)(2,1)} %copy-done.2, bf16[512,512]{1,0:T(8,128)(2,1)} %copy-done.21, bf16[512,512]{1,0:T(8,128)(2,1)S(1)} %get-tuple-element.23), kind=kOutput, calls=%fused_computation.13 | convolution fusion | flops 1346895872 | bytes 12845056 | tf_op jit(solution)/shard_map/dot_general | solution.py:236
  219.5 3.9 %fusion.15 = f32[1280,512]{1,0:T(8,128)S(1)} fusion(bf16[1024,512]{1,0:T(8,128)(2,1)} %collective-permute-done.9, bf16[1280,4096]{1,0:T(8,128)(2,1)} %copy-done.2), kind=kOutput, calls=%fused_computation.31 | convolution fusion | flops 1342177280 | bytes 6291456 | tf_op jit(solution)/shard_map/dot_general | solution.py:236
  225.0 5.8 %collective-permute-done.14 = bf16[1024,512]{1,0:T(8,128)(2,1)S(1)} collective-permute-done((bf16[1024,512]{1,0:T(8,128)(2,1)S(1)}, bf16[1024,512]{1,0:T(8,128)(2,1)S(1)}, u32[]{:S(2)}, u32[]{:S(2)}) %collective-permute-start.14) | collective-permute-done | bytes 1048608 | tf_op jit(solution)/shard_map/ppermute | solution.py:156
  234.5 22.5 %shard_map.83 = bf16[1280,512]{1,0:T(8,128)(2,1)S(1)} custom-call(s32[2,1,640]{2,1,0:T(1,128)S(1)} %broadcast_in_dim.413.q_ids, s32[1280,128]{1,0:T(8,128)S(1)} %broadcast_in_dim.415.k_ids, f32[8,640,128]{2,1,0:T(8,128)S(1)} %copy-done.5, bf16[1280,512]{1,0:T(8,128)(2,1)S(1)} %fusion.6.queries, bf16[1280,512]{1,0:T(8,128)(2,1)S(1)} %fusion.7.keys, ...), custom_call_target="tpu_custom_call" | custom-call | flops 3355443200 | bytes 10485760 | tf_op jit(solution)/shard_map/pallas_call | solution.py:81
  256.9 9.9 %all-gather.11.cloned.1.call-done = bf16[2048,512]{1,0:T(8,128)(2,1)} async-done(((bf16[1024,512]{1,0:T(8,128)(2,1)}), bf16[2048,512]{1,0:T(8,128)(2,1)}) %all-gather.11.cloned.1.call-update) | async-done | bytes 2097168 | tf_op jit(solution)/shard_map/all_gather | solution.py:189
  272.7 3.0 convolution_convert_fusion.3
  281.3 2.4 convolution_add_fusion.3
  283.7 17.5 %collective-permute-done.21 = bf16[1024,512]{1,0:T(8,128)(2,1)S(1)} collective-permute-done((bf16[1024,512]{1,0:T(8,128)(2,1)S(1)}, bf16[1024,512]{1,0:T(8,128)(2,1)S(1)}, u32[]{:S(2)}, u32[]{:S(2)}) %collective-permute-start.21) | collective-permute-done | bytes 1048608 | tf_op jit(solution)/shard_map/ppermute | solution.py:156
  308.3 17.8 %collective-permute-start.24 = (bf16[640,1024]{0,1:T(8,128)(2,1)S(1)}, bf16[640,1024]{0,1:T(8,128)(2,1)S(1)}, u32[]{:S(2)}, u32[]{:S(2)}) collective-permute-start(bf16[640,1024]{0,1:T(8,128)(2,1)S(1)} %pad_maximum_fusion.1), channel_id=1, source_target_pairs={{0,8},{4,12},{8,0},{12,4},{16,24},{20,28},{24,16},{28,20},{1,9},{5... | collective-permute-start | bytes 3932168 | tf_op jit(solution)/shard_map/ppermute | solution.py:156
  326.1 8.4 %collective-permute-done.18 = bf16[1280,512]{0,1:T(8,128)(2,1)S(1)} collective-permute-done((bf16[1280,512]{0,1:T(8,128)(2,1)S(1)}, bf16[1280,512]{0,1:T(8,128)(2,1)S(1)}, u32[]{:S(2)}, u32[]{:S(2)}) %collective-permute-start.18) | collective-permute-done | bytes 1310752 | tf_op jit(solution)/shard_map/ppermute | solution.py:156
  335.8 17.7 %collective-permute-start.19 = (bf16[640,512]{0,1:T(8,128)(2,1)}, bf16[640,512]{0,1:T(8,128)(2,1)}, u32[]{:S(2)}, u32[]{:S(2)}) collective-permute-start(bf16[640,512]{0,1:T(8,128)(2,1)} %slice.273), channel_id=1, source_target_pairs={{0,8},{4,12},{8,0},{12,4},{16,24},{20,28},{24,16},{28,20},{1,9},{5... | collective-permute-start | bytes 1966088 | tf_op jit(solution)/shard_map/ppermute | solution.py:156
  358.2 11.2 %collective-permute-done.19 = bf16[640,512]{0,1:T(8,128)(2,1)} collective-permute-done((bf16[640,512]{0,1:T(8,128)(2,1)}, bf16[640,512]{0,1:T(8,128)(2,1)}, u32[]{:S(2)}, u32[]{:S(2)}) %collective-permute-start.19) | collective-permute-done | bytes 655392 | tf_op jit(solution)/shard_map/ppermute | solution.py:156
  375.4 3.6 add_convert_fusion
  (186 shorter events, 70.1 us)
Async XLA Ops:
  6.5 89.2 %copy-start = (f32[32,16]{0,1:T(8,128)S(1)}, f32[32,16]{0,1:T(8,128)}, u32[]{:S(2)}) copy-start(f32[32,16]{0,1:T(8,128)} %param.10) | copy-start | bytes 6148
  6.5 114.3 %all-gather.5.cloned.1.call-start = ((), (), s32[]{:S(2)}) async-start(), calls=%async_computation | async-start | bytes 6553600 | tf_op jit(solution)/shard_map/all_gather | solution.py:206
  7.3 166.2 %all-gather.7.cloned.1.call-start = ((), (), s32[]{:S(2)}) async-start(), calls=%async_computation.1 | async-start | bytes 6553600 | tf_op jit(solution)/shard_map/all_gather | solution.py:206
  8.7 81.6 %copy-start.11 = (bf16[512,512]{1,0:T(8,128)(2,1)}, bf16[512,512]{1,0:T(8,128)(2,1)S(1)}, u32[]{:S(2)}) copy-start(bf16[512,512]{1,0:T(8,128)(2,1)S(1)} %get-tuple-element.72) | copy-start | bytes 1572868
  8.7 18.0 %collective-permute-start.2 = (bf16[512,512]{1,0:T(8,128)(2,1)S(1)}, bf16[512,512]{1,0:T(8,128)(2,1)S(1)}, u32[]{:S(2)}, u32[]{:S(2)}) collective-permute-start(bf16[512,512]{1,0:T(8,128)(2,1)S(1)} %get-tuple-element.21), channel_id=1, source_target_pairs={{0,24},{4,28},{8,16},{12,20},{16,8},{20,12},{24,0},{28,4},{1,25},{... | collective-permute-start | bytes 1572872 | tf_op jit(solution)/shard_map/ppermute | solution.py:156
  13.9 23.1 %collective-permute-start.1 = (bf16[512,512]{1,0:T(8,128)(2,1)S(1)}, bf16[512,512]{1,0:T(8,128)(2,1)S(1)}, u32[]{:S(2)}, u32[]{:S(2)}) collective-permute-start(bf16[512,512]{1,0:T(8,128)(2,1)S(1)} %get-tuple-element.70), channel_id=1, source_target_pairs={{0,8},{4,12},{8,0},{12,4},{16,24},{20,28},{24,16},{28,20},{1,9},{5... | collective-permute-start | bytes 1572872 | tf_op jit(solution)/shard_map/ppermute | solution.py:156
  37.1 30.9 %collective-permute-start.3 = (bf16[640,1024]{1,0:T(8,128)(2,1)S(1)}, bf16[640,1024]{1,0:T(8,128)(2,1)}, u32[]{:S(2)}, u32[]{:S(2)}) collective-permute-start(bf16[640,1024]{1,0:T(8,128)(2,1)S(1)} %copy-done.10), channel_id=1, source_target_pairs={{0,8},{4,12},{8,0},{12,4},{16,24},{20,28},{24,16},{28,20},{1,9},{5... | collective-permute-start | bytes 3932168 | tf_op jit(solution)/shard_map/ppermute | solution.py:156
  68.0 142.6 %all-gather.9.cloned.1.call-start = ((), (), s32[]{:S(2)}) async-start(), calls=%async_computation.2 | async-start | bytes 3145728 | tf_op jit(solution)/shard_map/all_gather | solution.py:189
  68.1 22.2 %collective-permute-start.4 = (bf16[512,512]{1,0:T(8,128)(2,1)}, bf16[512,512]{1,0:T(8,128)(2,1)S(1)}, u32[]{:S(2)}, u32[]{:S(2)}) collective-permute-start(bf16[512,512]{1,0:T(8,128)(2,1)} %copy-done.26), channel_id=1, source_target_pairs={{0,8},{4,12},{8,0},{12,4},{16,24},{20,28},{24,16},{28,20},{1,9},{5... | collective-permute-start | bytes 1572872 | tf_op jit(solution)/shard_map/ppermute | solution.py:156
  68.8 32.6 %collective-permute-start.6 = (bf16[512,512]{1,0:T(8,128)(2,1)S(1)}, bf16[512,512]{1,0:T(8,128)(2,1)}, u32[]{:S(2)}, u32[]{:S(2)}) collective-permute-start(bf16[512,512]{1,0:T(8,128)(2,1)S(1)} %get-tuple-element.72), channel_id=1, source_target_pairs={{0,16},{4,20},{8,24},{12,28},{16,0},{20,4},{24,8},{28,12},{1,17},{... | collective-permute-start | bytes 1572872 | tf_op jit(solution)/shard_map/ppermute | solution.py:156
  69.5 51.6 %collective-permute-start = (s32[1,640]{1,0:T(1,128)S(1)}, s32[1,640]{1,0:T(1,128)S(1)}, u32[]{:S(2)}, u32[]{:S(2)}) collective-permute-start(s32[1,640]{1,0:T(1,128)S(1)} %copy-done.33), channel_id=1, source_target_pairs={{0,8},{4,12},{8,0},{12,4},{16,24},{20,28},{24,16},{28,20},{1,9},{5... | collective-permute-start | bytes 7688 | tf_op jit(solution)/shard_map/ppermute | solution.py:156
  71.3 48.3 %collective-permute-start.9 = (bf16[1024,512]{1,0:T(8,128)(2,1)}, bf16[1024,512]{1,0:T(8,128)(2,1)}, u32[]{:S(2)}, u32[]{:S(2)}) collective-permute-start(bf16[1024,512]{1,0:T(8,128)(2,1)} %pad_maximum_fusion.3), channel_id=1, source_target_pairs={{0,4},{4,0},{8,12},{12,8},{16,20},{20,16},{24,28},{28,24},{1,5},{5... | collective-permute-start | bytes 3145736 | tf_op jit(solution)/shard_map/ppermute | solution.py:156
  91.4 29.5 %collective-permute-start.12 = (bf16[1024,512]{1,0:T(8,128)(2,1)}, bf16[1024,512]{1,0:T(8,128)(2,1)}, u32[]{:S(2)}, u32[]{:S(2)}) collective-permute-start(bf16[1024,512]{1,0:T(8,128)(2,1)} %pad_maximum_fusion.4), channel_id=1, source_target_pairs={{0,4},{4,0},{8,12},{12,8},{16,20},{20,16},{24,28},{28,24},{1,5},{5... | collective-permute-start | bytes 3145736 | tf_op jit(solution)/shard_map/ppermute | solution.py:156
  97.9 18.2 %collective-permute-start.5 = (bf16[512,512]{1,0:T(8,128)(2,1)}, bf16[512,512]{1,0:T(8,128)(2,1)S(1)}, u32[]{:S(2)}, u32[]{:S(2)}) collective-permute-start(bf16[512,512]{1,0:T(8,128)(2,1)} %get-tuple-element.22), channel_id=1, source_target_pairs={{0,8},{4,12},{8,0},{12,4},{16,24},{20,28},{24,16},{28,20},{1,9},{5... | collective-permute-start | bytes 1572872 | tf_op jit(solution)/shard_map/ppermute | solution.py:156
  101.5 66.6 %collective-permute-start.7 = (bf16[512,512]{1,0:T(8,128)(2,1)S(1)}, bf16[512,512]{1,0:T(8,128)(2,1)}, u32[]{:S(2)}, u32[]{:S(2)}) collective-permute-start(bf16[512,512]{1,0:T(8,128)(2,1)S(1)} %get-tuple-element.23), channel_id=1, source_target_pairs={{0,16},{4,20},{8,24},{12,28},{16,0},{20,4},{24,8},{28,12},{1,17},{... | collective-permute-start | bytes 1572872 | tf_op jit(solution)/shard_map/ppermute | solution.py:156
  116.1 53.1 %collective-permute-start.8 = (bf16[512,512]{1,0:T(8,128)(2,1)}, bf16[512,512]{1,0:T(8,128)(2,1)}, u32[]{:S(2)}, u32[]{:S(2)}) collective-permute-start(bf16[512,512]{1,0:T(8,128)(2,1)} %get-tuple-element.22), channel_id=1, source_target_pairs={{0,24},{4,28},{8,16},{12,20},{16,8},{20,12},{24,0},{28,4},{1,25},{... | collective-permute-start | bytes 1572872 | tf_op jit(solution)/shard_map/ppermute | solution.py:156
  119.6 52.8 %collective-permute-start.10 = (bf16[1024,512]{1,0:T(8,128)(2,1)}, bf16[1024,512]{1,0:T(8,128)(2,1)}, u32[]{:S(2)}, u32[]{:S(2)}) collective-permute-start(bf16[1024,512]{1,0:T(8,128)(2,1)} %pad_maximum_fusion.2), channel_id=1, source_target_pairs={{0,4},{4,0},{8,12},{12,8},{16,20},{20,16},{24,28},{28,24},{1,5},{5... | collective-permute-start | bytes 3145736 | tf_op jit(solution)/shard_map/ppermute | solution.py:156
  120.9 49.5 %collective-permute-start.15 = (bf16[512,512]{1,0:T(8,128)(2,1)}, bf16[512,512]{1,0:T(8,128)(2,1)S(1)}, u32[]{:S(2)}, u32[]{:S(2)}) collective-permute-start(bf16[512,512]{1,0:T(8,128)(2,1)} %get-tuple-element.30), channel_id=1, source_target_pairs={{0,8},{4,12},{8,0},{12,4},{16,24},{20,28},{24,16},{28,20},{1,9},{5... | collective-permute-start | bytes 1572872 | tf_op jit(solution)/shard_map/ppermute | solution.py:156
  120.9 145.9 %all-gather.11.cloned.1.call-start = ((), (), s32[]{:S(2)}) async-start(), calls=%async_computation.3 | async-start | bytes 3145728 | tf_op jit(solution)/shard_map/all_gather | solution.py:189
  121.1 63.7 %collective-permute-start.13 = (bf16[1024,512]{1,0:T(8,128)(2,1)}, bf16[1024,512]{1,0:T(8,128)(2,1)}, u32[]{:S(2)}, u32[]{:S(2)}) collective-permute-start(bf16[1024,512]{1,0:T(8,128)(2,1)} %copy-done.31), channel_id=1, source_target_pairs={{0,4},{4,0},{8,12},{12,8},{16,20},{20,16},{24,28},{28,24},{1,5},{5... | collective-permute-start | bytes 3145736 | tf_op jit(solution)/shard_map/ppermute | solution.py:156
  172.4 32.0 %collective-permute-start.11 = (bf16[1024,512]{1,0:T(8,128)(2,1)}, bf16[1024,512]{1,0:T(8,128)(2,1)}, u32[]{:S(2)}, u32[]{:S(2)}) collective-permute-start(bf16[1024,512]{1,0:T(8,128)(2,1)} %copy-done.29), channel_id=1, source_target_pairs={{0,4},{4,0},{8,12},{12,8},{16,20},{20,16},{24,28},{28,24},{1,5},{5... | collective-permute-start | bytes 3145736 | tf_op jit(solution)/shard_map/ppermute | solution.py:156
  184.9 91.3 %collective-permute-start.20 = (bf16[1024,512]{1,0:T(8,128)(2,1)}, bf16[1024,512]{1,0:T(8,128)(2,1)}, u32[]{:S(2)}, u32[]{:S(2)}) collective-permute-start(bf16[1024,512]{1,0:T(8,128)(2,1)} %pad_maximum_fusion.5), channel_id=1, source_target_pairs={{0,4},{4,0},{8,12},{12,8},{16,20},{20,16},{24,28},{28,24},{1,5},{5... | collective-permute-start | bytes 3145736 | tf_op jit(solution)/shard_map/ppermute | solution.py:156
  212.0 18.7 %collective-permute-start.14 = (bf16[1024,512]{1,0:T(8,128)(2,1)S(1)}, bf16[1024,512]{1,0:T(8,128)(2,1)S(1)}, u32[]{:S(2)}, u32[]{:S(2)}) collective-permute-start(bf16[1024,512]{1,0:T(8,128)(2,1)S(1)} %constant_dynamic-slice_fusion.3), channel_id=1, source_target_pairs={{0,4},{4,0},{8,12},{12,8},{16,20},{20,16},{24,28},{28,24},{1,5},{5... | collective-permute-start | bytes 3145736 | tf_op jit(solution)/shard_map/ppermute | solution.py:156
  272.7 6.3 %collective-permute-start.17 = (bf16[1280,512]{0,1:T(8,128)(2,1)}, bf16[1280,512]{0,1:T(8,128)(2,1)}, u32[]{:S(2)}, u32[]{:S(2)}) collective-permute-start(bf16[1280,512]{0,1:T(8,128)(2,1)} %convolution_convert_fusion.2), channel_id=1, source_target_pairs={{0,1},{1,0},{2,3},{3,2},{4,5},{5,4},{6,7},{7,6},{8,9},{9,8},{10,11... | collective-permute-start | bytes 3932168 | tf_op jit(solution)/shard_map/ppermute | solution.py:156
  275.6 5.7 %collective-permute-start.16 = (bf16[1280,512]{0,1:T(8,128)(2,1)}, bf16[1280,512]{0,1:T(8,128)(2,1)}, u32[]{:S(2)}, u32[]{:S(2)}) collective-permute-start(bf16[1280,512]{0,1:T(8,128)(2,1)} %convolution_convert_fusion.3), channel_id=1, source_target_pairs={{0,1},{1,0},{2,3},{3,2},{4,5},{5,4},{6,7},{7,6},{8,9},{9,8},{10,11... | collective-permute-start | bytes 3932168 | tf_op jit(solution)/shard_map/ppermute | solution.py:156
  276.2 25.1 %collective-permute-start.21 = (bf16[1024,512]{1,0:T(8,128)(2,1)S(1)}, bf16[1024,512]{1,0:T(8,128)(2,1)S(1)}, u32[]{:S(2)}, u32[]{:S(2)}) collective-permute-start(bf16[1024,512]{1,0:T(8,128)(2,1)S(1)} %constant_dynamic-slice_fusion), channel_id=1, source_target_pairs={{0,4},{4,0},{8,12},{12,8},{16,20},{20,16},{24,28},{28,24},{1,5},{5... | collective-permute-start | bytes 3145736 | tf_op jit(solution)/shard_map/ppermute | solution.py:156
  302.2 3.1 collective-permute-start.22
  303.2 4.0 %collective-permute-start.23 = (bf16[1280,512]{0,1:T(8,128)(2,1)S(1)}, bf16[1280,512]{0,1:T(8,128)(2,1)S(1)}, u32[]{:S(2)}, u32[]{:S(2)}) collective-permute-start(bf16[1280,512]{0,1:T(8,128)(2,1)S(1)} %convolution_convert_fusion), channel_id=1, source_target_pairs={{0,1},{1,0},{2,3},{3,2},{4,5},{5,4},{6,7},{7,6},{8,9},{9,8},{10,11... | collective-permute-start | bytes 3932168 | tf_op jit(solution)/shard_map/ppermute | solution.py:156
  303.8 30.8 %collective-permute-start.18 = (bf16[1280,512]{0,1:T(8,128)(2,1)S(1)}, bf16[1280,512]{0,1:T(8,128)(2,1)S(1)}, u32[]{:S(2)}, u32[]{:S(2)}) collective-permute-start(bf16[1280,512]{0,1:T(8,128)(2,1)S(1)} %convolution_add_fusion.2), channel_id=1, source_target_pairs={{0,2},{1,3},{2,0},{3,1},{4,6},{5,7},{6,4},{7,5},{8,10},{9,11},{10,... | collective-permute-start | bytes 3932168 | tf_op jit(solution)/shard_map/ppermute | solution.py:156
  308.3 47.3 %collective-permute-start.24 = (bf16[640,1024]{0,1:T(8,128)(2,1)S(1)}, bf16[640,1024]{0,1:T(8,128)(2,1)S(1)}, u32[]{:S(2)}, u32[]{:S(2)}) collective-permute-start(bf16[640,1024]{0,1:T(8,128)(2,1)S(1)} %pad_maximum_fusion.1), channel_id=1, source_target_pairs={{0,8},{4,12},{8,0},{12,4},{16,24},{20,28},{24,16},{28,20},{1,9},{5... | collective-permute-start | bytes 3932168 | tf_op jit(solution)/shard_map/ppermute | solution.py:156
  335.8 33.5 %collective-permute-start.19 = (bf16[640,512]{0,1:T(8,128)(2,1)}, bf16[640,512]{0,1:T(8,128)(2,1)}, u32[]{:S(2)}, u32[]{:S(2)}) collective-permute-start(bf16[640,512]{0,1:T(8,128)(2,1)} %slice.273), channel_id=1, source_target_pairs={{0,8},{4,12},{8,0},{12,4},{16,24},{20,28},{24,16},{28,20},{1,9},{5... | collective-permute-start | bytes 1966088 | tf_op jit(solution)/shard_map/ppermute | solution.py:156
  356.9 16.0 %collective-permute-start.25 = (bf16[640,512]{0,1:T(8,128)(2,1)}, bf16[640,512]{0,1:T(8,128)(2,1)S(1)}, u32[]{:S(2)}, u32[]{:S(2)}) collective-permute-start(bf16[640,512]{0,1:T(8,128)(2,1)} %fusion.30), channel_id=1, source_target_pairs={{0,2},{1,3},{2,0},{3,1},{4,6},{5,7},{6,4},{7,5},{8,10},{9,11},{10,... | collective-permute-start | bytes 1966088 | tf_op jit(solution)/shard_map/ppermute | solution.py:156
  (43 other events, 674.3 us)
Sparse Core Ops, SparseCore 0:
  8.9 43.1 all-gather.4
  68.2 38.7 all-gather.6
  121.0 73.3 all-gather.8
  195.8 71.0 all-gather.10

commit v2 on v1

--- a/solution.py
+++ b/solution.py
@@ -202,9 +202,9 @@
 
     peer_tokens = paced(tokens, 2, pair_line, 1, far_line[0])
     peer_ids = swap(segments, 2)
-    own_all, peer_all = [
-        lax.all_gather(part, "hidden", axis=1, tiled=True) for part in (tokens, peer_tokens)
-    ]
+    own_all = lax.all_gather(tokens, "hidden", axis=1, tiled=True)
+    value_far = gathered(after(value_close, own_all))
+    peer_all = lax.all_gather(after(peer_tokens, (value_far, far_line[1])), "hidden", axis=1, tiled=True)
 
     key_close = close_by(key_parts)
     query_close = close_by(query_parts)
@@ -213,7 +213,6 @@
 
     value_near = along_x(value_close)
     key_near = along_x(key_close)
-    value_far = gathered(after(value_close, own_all))
     query_near = along_x(query_close)
     key_rest = along_x(key_far)
     query_rest = along_x(query_far)
@@ -241,7 +240,7 @@
     queries = project(query_close, query_far, query_near, query_rest)
     out_far = gathered(after(out_close, normed))
     out_near = along_x(out_close, normed)
-    value_rest = along_x(value_far, normed)
+    value_rest = along_x(value_far)
     values = project(value_close, value_far, value_near, value_rest)
     out_rest = along_x(out_far, values)
     ids = jnp.concatenate([segments, peer_ids], axis=0)

time: 390 us -> 479 us (1.23)
  waiting for transfers between devices: 173 us -> 231 us
  starting transfers between devices: 63.2 us -> 92.8 us
  local copies, waits for them, and re-layouts: 25.4 us -> 33 us
    ppermute x26, starting transfers between devices: 62.9 us -> 92.7 us  [swap(): return lax.ppermute(value, axis, [(i, i ^ step) for i in range(count)])]
    all_gather x2, waiting for transfers between devices: 0.01 us -> 27.4 us  [the longest x1 27.4 us: per_device(): own_all = lax.all_gather(tokens, 'hidden', axis=1, tiled=True)]
    ppermute x26, waiting for transfers between devices: 162 us -> 183 us  [swap(): return lax.ppermute(value, axis, [(i, i ^ step) for i in range(count)])]
    all_gather x2, waiting for transfers between devices: 9.93 us -> 20.3 us  [gathered(): lax.all_gather(close, 'batch', axis=0, tiled=True, axis_index_groups=groups)]
    unnamed x93 -> x47, local copies, waits for them, and re-layouts: 10.9 us -> 15.4 us
  transfers between devices with their start and end apart: 30 -> 30, of which waited for: 15 -> 19; matrix products, arithmetic and copies ran while one was open for 24% -> 19% of each run, Pallas kernels for 7% -> 6%
where the time goes in v2:
time: 479 us; the launch traced here: 476 us
  waiting for transfers between devices  231 us (48%)
  starting transfers between devices  92.8 us (19%)
  matrix products  49.3 us (10%)
  local copies, waits for them, and re-layouts  33 us (7%)
  Pallas kernels  28.8 us (6%)
  other arithmetic  27 us (6%)
  between operations  13.8 us (3%)
    ppermute x26, waiting for transfers between devices, swap(): return lax.ppermute(value, axis, [(i, i ^ step) for i in range(count)])  183 us
    ppermute x26, starting transfers between devices, swap(): return lax.ppermute(value, axis, [(i, i ^ step) for i in range(count)])  92.7 us
    dot_general x12, matrix products, project(): term = jnp.dot(part, rows, preferred_element_type=jnp.float32)  35.9 us
    all_gather x1, waiting for transfers between devices, per_device(): own_all = lax.all_gather(tokens, 'hidden', axis=1, tiled=True)  27.4 us
    pallas_call x1, Pallas kernels, attend(): pl.pallas_call(functools.partial(attention_kernel, width), grid=(groups,...  22.5 us
    all_gather x2, waiting for transfers between devices, gathered(): lax.all_gather(close, 'batch', axis=0, tiled=True, axis_index_groups=groups)  20.3 us
    unnamed x47, local copies, waits for them, and re-layouts  15.4 us
    dot_general x8, matrix products, block(): return jnp.dot(attended, chosen, preferred_element_type=jnp.float32)  13.4 us
  transfers between devices with their start and end apart: 30, of which 19 were waited for; matrix products, arithmetic and copies ran while one was open for 19% of the time, Pallas kernels for 6%

profile of v2, /device:TPU:0, one launch (start us, length us, event | category | flops | bytes accessed | tf_op | source)
XLA Modules:
  0.0 476.0 jit_solution(14326554065449807511)
XLA Ops:
  8.6 3.1 collective-permute-start.1
  11.7 11.9 %collective-permute-done.1 = bf16[512,512]{1,0:T(8,128)(2,1)S(1)} collective-permute-done((bf16[512,512]{1,0:T(8,128)(2,1)S(1)}, bf16[512,512]{1,0:T(8,128)(2,1)S(1)}, u32[]{:S(2)}, u32[]{:S(2)}) %collective-permute-start.1) | collective-permute-done | bytes 524320 | tf_op jit(solution)/shard_map/ppermute | solution.py:156
  24.6 27.4 %all-gather.5.cloned.1.call-done.own = bf16[640,4096]{1,0:T(8,128)(2,1)} async-done(((bf16[640,1024]{1,0:T(8,128)(2,1)}), bf16[640,4096]{1,0:T(8,128)(2,1)}) %all-gather.5.cloned.1.call-update) | async-done | bytes 5242896 | tf_op jit(solution)/shard_map/all_gather | solution.py:205
  53.4 3.4 collective-permute-start.2
  56.8 18.8 %collective-permute-done.2 = bf16[512,512]{1,0:T(8,128)(2,1)S(1)} collective-permute-done((bf16[512,512]{1,0:T(8,128)(2,1)S(1)}, bf16[512,512]{1,0:T(8,128)(2,1)S(1)}, u32[]{:S(2)}, u32[]{:S(2)}) %collective-permute-start.2) | collective-permute-done | bytes 524320 | tf_op jit(solution)/shard_map/ppermute | solution.py:156
  75.6 38.1 %collective-permute-start.3 = (bf16[640,1024]{1,0:T(8,128)(2,1)S(1)}, bf16[640,1024]{1,0:T(8,128)(2,1)}, u32[]{:S(2)}, u32[]{:S(2)}) collective-permute-start(bf16[640,1024]{1,0:T(8,128)(2,1)S(1)} %copy-done.10), channel_id=1, source_target_pairs={{0,8},{4,12},{8,0},{12,4},{16,24},{20,28},{24,16},{28,20},{1,9},{5... | collective-permute-start | bytes 3932168 | tf_op jit(solution)/shard_map/ppermute | solution.py:156
  113.7 19.9 %all-gather.7.cloned.1.call-done = bf16[2048,512]{1,0:T(8,128)(2,1)} async-done(((bf16[1024,512]{1,0:T(8,128)(2,1)}), bf16[2048,512]{1,0:T(8,128)(2,1)}) %all-gather.7.cloned.1.call-update) | async-done | bytes 2097168 | tf_op jit(solution)/shard_map/all_gather | solution.py:189
  136.0 15.3 %collective-permute-done.4 = bf16[512,512]{1,0:T(8,128)(2,1)} collective-permute-done((bf16[512,512]{1,0:T(8,128)(2,1)S(1)}, bf16[512,512]{1,0:T(8,128)(2,1)}, u32[]{:S(2)}, u32[]{:S(2)}) %collective-permute-start.4) | collective-permute-done | bytes 524320 | tf_op jit(solution)/shard_map/ppermute | solution.py:156
  151.2 12.7 %collective-permute-done.3 = bf16[640,1024]{1,0:T(8,128)(2,1)} collective-permute-done((bf16[640,1024]{1,0:T(8,128)(2,1)S(1)}, bf16[640,1024]{1,0:T(8,128)(2,1)}, u32[]{:S(2)}, u32[]{:S(2)}) %collective-permute-start.3) | collective-permute-done | bytes 1310752 | tf_op jit(solution)/shard_map/ppermute | solution.py:156
  167.7 10.3 %collective-permute-done.5 = bf16[512,512]{1,0:T(8,128)(2,1)S(1)} collective-permute-done((bf16[512,512]{1,0:T(8,128)(2,1)}, bf16[512,512]{1,0:T(8,128)(2,1)S(1)}, u32[]{:S(2)}, u32[]{:S(2)}) %collective-permute-start.5) | collective-permute-done | bytes 524320 | tf_op jit(solution)/shard_map/ppermute | solution.py:156
  183.1 8.2 %collective-permute-done.6 = bf16[512,512]{1,0:T(8,128)(2,1)} collective-permute-done((bf16[512,512]{1,0:T(8,128)(2,1)}, bf16[512,512]{1,0:T(8,128)(2,1)}, u32[]{:S(2)}, u32[]{:S(2)}) %collective-permute-start.6) | collective-permute-done | bytes 524320 | tf_op jit(solution)/shard_map/ppermute | solution.py:156
  199.6 30.0 %collective-permute-done.7 = bf16[512,512]{1,0:T(8,128)(2,1)S(1)} collective-permute-done((bf16[512,512]{1,0:T(8,128)(2,1)S(1)}, bf16[512,512]{1,0:T(8,128)(2,1)S(1)}, u32[]{:S(2)}, u32[]{:S(2)}) %collective-permute-start.7) | collective-permute-done | bytes 524320 | tf_op jit(solution)/shard_map/ppermute | solution.py:156
  232.9 10.4 %collective-permute-start.15 = (bf16[512,512]{1,0:T(8,128)(2,1)}, bf16[512,512]{1,0:T(8,128)(2,1)}, u32[]{:S(2)}, u32[]{:S(2)}) collective-permute-start(bf16[512,512]{1,0:T(8,128)(2,1)} %get-tuple-element.32), channel_id=1, source_target_pairs={{0,8},{4,12},{8,0},{12,4},{16,24},{20,28},{24,16},{28,20},{1,9},{5... | collective-permute-start | bytes 1572872 | tf_op jit(solution)/shard_map/ppermute | solution.py:156
  245.8 10.8 %select_select_fusion.bias = f32[8,640,128]{2,1,0:T(8,128)} fusion(f32[8]{0:T(128)S(1)} %get-tuple-element.38, f32[8]{0:T(128)S(1)} %get-tuple-element.39, f32[8]{0:T(128)S(1)} %get-tuple-element.40, f32[8]{0:T(128)S(1)} %get-tuple-element.41, f32[8]{0:T(128)S(1)} %get-tuple-element.42, f32[8]{0:T(128)S(1)} %get-tuple-element.43, ...), kind=kLoop, calls=%fused_computation.23 | loop fusion | flops 20971520 | bytes 5243904 | tf_op jit(solution)/shard_map/jit(_where)/select_n | solution.py:35
  263.2 18.1 %collective-permute-done.11 = bf16[1024,512]{1,0:T(8,128)(2,1)} collective-permute-done((bf16[1024,512]{1,0:T(8,128)(2,1)}, bf16[1024,512]{1,0:T(8,128)(2,1)}, u32[]{:S(2)}, u32[]{:S(2)}) %collective-permute-start.11) | collective-permute-done | bytes 1048608 | tf_op jit(solution)/shard_map/ppermute | solution.py:156
  286.8 6.4 %shard_map.82 = bf16[1280,4096]{1,0:T(8,128)(2,1)S(1)} custom-call(s32[8]{0:T(128)S(1)} %stack.45.sources, f32[1,4096]{1,0:T(1,128)S(1)} %bitcast.33, bf16[640,4096]{1,0:T(8,128)(2,1)S(1)} %copy-done.3, bf16[640,4096]{1,0:T(8,128)(2,1)S(1)} %copy-done.4), custom_call_target="tpu_custom_call" | custom-call | flops 41943040 | bytes 20971520 | tf_op jit(solution)/shard_map/pallas_call | solution.py:121
  293.1 4.0 copy-done.2
  297.1 3.0 fusion.21
  300.1 3.7 fusion.23
  303.9 3.7 fusion.25
  314.7 3.0 fusion.17
  319.2 7.0 %collective-permute-done.14 = bf16[1024,512]{1,0:T(8,128)(2,1)} collective-permute-done((bf16[1024,512]{1,0:T(8,128)(2,1)}, bf16[1024,512]{1,0:T(8,128)(2,1)}, u32[]{:S(2)}, u32[]{:S(2)}) %collective-permute-start.14) | collective-permute-done | bytes 1048608 | tf_op jit(solution)/shard_map/ppermute | solution.py:156
  326.2 4.3 fusion.9
  330.4 3.6 fusion.8.values
  341.9 22.5 %shard_map.83 = bf16[1280,512]{1,0:T(8,128)(2,1)S(1)} custom-call(s32[2,1,640]{2,1,0:T(1,128)S(1)} %broadcast_in_dim.413.q_ids, s32[1280,128]{1,0:T(8,128)S(1)} %broadcast_in_dim.415.k_ids, f32[8,640,128]{2,1,0:T(8,128)S(1)} %copy-done.5, bf16[1280,512]{1,0:T(8,128)(2,1)S(1)} %fusion.6.queries, bf16[1280,512]{1,0:T(8,128)(2,1)S(1)} %fusion.7.keys, ...), custom_call_target="tpu_custom_call" | custom-call | flops 3355443200 | bytes 10485760 | tf_op jit(solution)/shard_map/pallas_call | solution.py:81
  370.6 3.0 convolution_convert_fusion.3
  381.7 17.5 %collective-permute-done.21 = bf16[1024,512]{1,0:T(8,128)(2,1)S(1)} collective-permute-done((bf16[1024,512]{1,0:T(8,128)(2,1)S(1)}, bf16[1024,512]{1,0:T(8,128)(2,1)S(1)}, u32[]{:S(2)}, u32[]{:S(2)}) %collective-permute-start.21) | collective-permute-done | bytes 1048608 | tf_op jit(solution)/shard_map/ppermute | solution.py:156
  406.3 10.1 %collective-permute-start.24 = (bf16[640,1024]{0,1:T(8,128)(2,1)S(1)}, bf16[640,1024]{0,1:T(8,128)(2,1)S(1)}, u32[]{:S(2)}, u32[]{:S(2)}) collective-permute-start(bf16[640,1024]{0,1:T(8,128)(2,1)S(1)} %pad_maximum_fusion.1), channel_id=1, source_target_pairs={{0,8},{4,12},{8,0},{12,4},{16,24},{20,28},{24,16},{28,20},{1,9},{5... | collective-permute-start | bytes 3932168 | tf_op jit(solution)/shard_map/ppermute | solution.py:156
  416.4 16.1 %collective-permute-done.18 = bf16[1280,512]{0,1:T(8,128)(2,1)S(1)} collective-permute-done((bf16[1280,512]{0,1:T(8,128)(2,1)S(1)}, bf16[1280,512]{0,1:T(8,128)(2,1)S(1)}, u32[]{:S(2)}, u32[]{:S(2)}) %collective-permute-start.18) | collective-permute-done | bytes 1310752 | tf_op jit(solution)/shard_map/ppermute | solution.py:156
  433.8 10.0 %collective-permute-start.19 = (bf16[640,512]{0,1:T(8,128)(2,1)}, bf16[640,512]{0,1:T(8,128)(2,1)}, u32[]{:S(2)}, u32[]{:S(2)}) collective-permute-start(bf16[640,512]{0,1:T(8,128)(2,1)} %slice.273), channel_id=1, source_target_pairs={{0,8},{4,12},{8,0},{12,4},{16,24},{20,28},{24,16},{28,20},{1,9},{5... | collective-permute-start | bytes 1966088 | tf_op jit(solution)/shard_map/ppermute | solution.py:156
  447.8 11.8 %collective-permute-done.19 = bf16[640,512]{0,1:T(8,128)(2,1)} collective-permute-done((bf16[640,512]{0,1:T(8,128)(2,1)}, bf16[640,512]{0,1:T(8,128)(2,1)}, u32[]{:S(2)}, u32[]{:S(2)}) %collective-permute-start.19) | collective-permute-done | bytes 655392 | tf_op jit(solution)/shard_map/ppermute | solution.py:156
  465.7 3.6 add_convert_fusion
  (139 shorter events, 90.6 us)
Async XLA Ops:
  6.5 173.5 %copy-start = (f32[32,16]{0,1:T(8,128)S(1)}, f32[32,16]{0,1:T(8,128)}, u32[]{:S(2)}) copy-start(f32[32,16]{0,1:T(8,128)} %param.10) | copy-start | bytes 6148
  6.5 45.6 %all-gather.5.cloned.1.call-start = ((), (), s32[]{:S(2)}) async-start(), calls=%async_computation | async-start | bytes 6553600 | tf_op jit(solution)/shard_map/all_gather | solution.py:205
  7.3 126.4 %all-gather.7.cloned.1.call-start = ((), (), s32[]{:S(2)}) async-start(), calls=%async_computation.1 | async-start | bytes 3145728 | tf_op jit(solution)/shard_map/all_gather | solution.py:189
  8.6 15.0 %collective-permute-start.1 = (bf16[512,512]{1,0:T(8,128)(2,1)S(1)}, bf16[512,512]{1,0:T(8,128)(2,1)S(1)}, u32[]{:S(2)}, u32[]{:S(2)}) collective-permute-start(bf16[512,512]{1,0:T(8,128)(2,1)S(1)} %get-tuple-element.72), channel_id=1, source_target_pairs={{0,8},{4,12},{8,0},{12,4},{16,24},{20,28},{24,16},{28,20},{1,9},{5... | collective-permute-start | bytes 1572872 | tf_op jit(solution)/shard_map/ppermute | solution.py:156
  52.1 229.7 %all-gather.9.cloned.1.call-start = ((), (), s32[]{:S(2)}) async-start(), calls=%async_computation.2 | async-start | bytes 6553600 | tf_op jit(solution)/shard_map/all_gather | solution.py:207
  53.4 22.2 %collective-permute-start.2 = (bf16[512,512]{1,0:T(8,128)(2,1)S(1)}, bf16[512,512]{1,0:T(8,128)(2,1)S(1)}, u32[]{:S(2)}, u32[]{:S(2)}) collective-permute-start(bf16[512,512]{1,0:T(8,128)(2,1)S(1)} %get-tuple-element.24), channel_id=1, source_target_pairs={{0,24},{4,28},{8,16},{12,20},{16,8},{20,12},{24,0},{28,4},{1,25},{... | collective-permute-start | bytes 1572872 | tf_op jit(solution)/shard_map/ppermute | solution.py:156
  75.6 92.1 %copy-start.14 = (bf16[512,512]{1,0:T(8,128)(2,1)}, bf16[512,512]{1,0:T(8,128)(2,1)S(1)}, u32[]{:S(2)}) copy-start(bf16[512,512]{1,0:T(8,128)(2,1)S(1)} %collective-permute-done.2) | copy-start | bytes 1572868
  75.6 88.3 %collective-permute-start.3 = (bf16[640,1024]{1,0:T(8,128)(2,1)S(1)}, bf16[640,1024]{1,0:T(8,128)(2,1)}, u32[]{:S(2)}, u32[]{:S(2)}) collective-permute-start(bf16[640,1024]{1,0:T(8,128)(2,1)S(1)} %copy-done.10), channel_id=1, source_target_pairs={{0,8},{4,12},{8,0},{12,4},{16,24},{20,28},{24,16},{28,20},{1,9},{5... | collective-permute-start | bytes 3932168 | tf_op jit(solution)/shard_map/ppermute | solution.py:156
  113.7 37.5 %collective-permute-start.4 = (bf16[512,512]{1,0:T(8,128)(2,1)S(1)}, bf16[512,512]{1,0:T(8,128)(2,1)}, u32[]{:S(2)}, u32[]{:S(2)}) collective-permute-start(bf16[512,512]{1,0:T(8,128)(2,1)S(1)} %get-tuple-element.74), channel_id=1, source_target_pairs={{0,16},{4,20},{8,24},{12,28},{16,0},{20,4},{24,8},{28,12},{1,17},{... | collective-permute-start | bytes 1572872 | tf_op jit(solution)/shard_map/ppermute | solution.py:156
  164.0 200.9 %all-gather.11.cloned.1.call-start = ((), (), s32[]{:S(2)}) async-start(), calls=%async_computation.3 | async-start | bytes 3145728 | tf_op jit(solution)/shard_map/all_gather | solution.py:189
  164.0 14.0 %collective-permute-start.5 = (bf16[512,512]{1,0:T(8,128)(2,1)}, bf16[512,512]{1,0:T(8,128)(2,1)S(1)}, u32[]{:S(2)}, u32[]{:S(2)}) collective-permute-start(bf16[512,512]{1,0:T(8,128)(2,1)} %copy-done.15), channel_id=1, source_target_pairs={{0,8},{4,12},{8,0},{12,4},{16,24},{20,28},{24,16},{28,20},{1,9},{5... | collective-permute-start | bytes 1572872 | tf_op jit(solution)/shard_map/ppermute | solution.py:156
  164.1 28.4 %collective-permute-start.9 = (bf16[1024,512]{1,0:T(8,128)(2,1)}, bf16[1024,512]{1,0:T(8,128)(2,1)}, u32[]{:S(2)}, u32[]{:S(2)}) collective-permute-start(bf16[1024,512]{1,0:T(8,128)(2,1)} %pad_maximum_fusion.2), channel_id=1, source_target_pairs={{0,4},{4,0},{8,12},{12,8},{16,20},{20,16},{24,28},{28,24},{1,5},{5... | collective-permute-start | bytes 3145736 | tf_op jit(solution)/shard_map/ppermute | solution.py:156
  178.0 13.3 %collective-permute-start.6 = (bf16[512,512]{1,0:T(8,128)(2,1)}, bf16[512,512]{1,0:T(8,128)(2,1)}, u32[]{:S(2)}, u32[]{:S(2)}) collective-permute-start(bf16[512,512]{1,0:T(8,128)(2,1)} %get-tuple-element.25), channel_id=1, source_target_pairs={{0,8},{4,12},{8,0},{12,4},{16,24},{20,28},{24,16},{28,20},{1,9},{5... | collective-permute-start | bytes 1572872 | tf_op jit(solution)/shard_map/ppermute | solution.py:156
  178.3 78.4 %collective-permute-start = (s32[1,640]{1,0:T(1,128)S(1)}, s32[1,640]{1,0:T(1,128)S(1)}, u32[]{:S(2)}, u32[]{:S(2)}) collective-permute-start(s32[1,640]{1,0:T(1,128)S(1)} %copy-done.16), channel_id=1, source_target_pairs={{0,8},{4,12},{8,0},{12,4},{16,24},{20,28},{24,16},{28,20},{1,9},{5... | collective-permute-start | bytes 7688 | tf_op jit(solution)/shard_map/ppermute | solution.py:156
  192.5 50.9 %collective-permute-start.10 = (bf16[1024,512]{1,0:T(8,128)(2,1)S(1)}, bf16[1024,512]{1,0:T(8,128)(2,1)S(1)}, u32[]{:S(2)}, u32[]{:S(2)}) collective-permute-start(bf16[1024,512]{1,0:T(8,128)(2,1)S(1)} %pad_maximum_fusion.3), channel_id=1, source_target_pairs={{0,4},{4,0},{8,12},{12,8},{16,20},{20,16},{24,28},{28,24},{1,5},{5... | collective-permute-start | bytes 3145736 | tf_op jit(solution)/shard_map/ppermute | solution.py:156
  194.0 35.6 %collective-permute-start.7 = (bf16[512,512]{1,0:T(8,128)(2,1)S(1)}, bf16[512,512]{1,0:T(8,128)(2,1)S(1)}, u32[]{:S(2)}, u32[]{:S(2)}) collective-permute-start(bf16[512,512]{1,0:T(8,128)(2,1)S(1)} %get-tuple-element.26), channel_id=1, source_target_pairs={{0,16},{4,20},{8,24},{12,28},{16,0},{20,4},{24,8},{28,12},{1,17},{... | collective-permute-start | bytes 1572872 | tf_op jit(solution)/shard_map/ppermute | solution.py:156
  195.5 34.9 %collective-permute-start.8 = (bf16[512,512]{1,0:T(8,128)(2,1)}, bf16[512,512]{1,0:T(8,128)(2,1)S(1)}, u32[]{:S(2)}, u32[]{:S(2)}) collective-permute-start(bf16[512,512]{1,0:T(8,128)(2,1)} %get-tuple-element.25), channel_id=1, source_target_pairs={{0,24},{4,28},{8,16},{12,20},{16,8},{20,12},{24,0},{28,4},{1,25},{... | collective-permute-start | bytes 1572872 | tf_op jit(solution)/shard_map/ppermute | solution.py:156
  232.3 28.1 %collective-permute-start.12 = (bf16[1024,512]{1,0:T(8,128)(2,1)}, bf16[1024,512]{1,0:T(8,128)(2,1)}, u32[]{:S(2)}, u32[]{:S(2)}) collective-permute-start(bf16[1024,512]{1,0:T(8,128)(2,1)} %pad_maximum_fusion.4), channel_id=1, source_target_pairs={{0,4},{4,0},{8,12},{12,8},{16,20},{20,16},{24,28},{28,24},{1,5},{5... | collective-permute-start | bytes 3145736 | tf_op jit(solution)/shard_map/ppermute | solution.py:156
  232.9 28.2 %collective-permute-start.15 = (bf16[512,512]{1,0:T(8,128)(2,1)}, bf16[512,512]{1,0:T(8,128)(2,1)}, u32[]{:S(2)}, u32[]{:S(2)}) collective-permute-start(bf16[512,512]{1,0:T(8,128)(2,1)} %get-tuple-element.32), channel_id=1, source_target_pairs={{0,8},{4,12},{8,0},{12,4},{16,24},{20,28},{24,16},{28,20},{1,9},{5... | collective-permute-start | bytes 1572872 | tf_op jit(solution)/shard_map/ppermute | solution.py:156
  244.4 36.9 %collective-permute-start.11 = (bf16[1024,512]{1,0:T(8,128)(2,1)}, bf16[1024,512]{1,0:T(8,128)(2,1)}, u32[]{:S(2)}, u32[]{:S(2)}) collective-permute-start(bf16[1024,512]{1,0:T(8,128)(2,1)} %constant_dynamic-update-slice_fusion), channel_id=1, source_target_pairs={{0,4},{4,0},{8,12},{12,8},{16,20},{20,16},{24,28},{28,24},{1,5},{5... | collective-permute-start | bytes 3145736 | tf_op jit(solution)/shard_map/ppermute | solution.py:156
  260.5 47.1 %collective-permute-start.13 = (bf16[1024,512]{1,0:T(8,128)(2,1)}, bf16[1024,512]{1,0:T(8,128)(2,1)}, u32[]{:S(2)}, u32[]{:S(2)}) collective-permute-start(bf16[1024,512]{1,0:T(8,128)(2,1)} %constant_dynamic-update-slice_fusion.2), channel_id=1, source_target_pairs={{0,4},{4,0},{8,12},{12,8},{16,20},{20,16},{24,28},{28,24},{1,5},{5... | collective-permute-start | bytes 3145736 | tf_op jit(solution)/shard_map/ppermute | solution.py:156
  281.2 44.9 %collective-permute-start.14 = (bf16[1024,512]{1,0:T(8,128)(2,1)}, bf16[1024,512]{1,0:T(8,128)(2,1)}, u32[]{:S(2)}, u32[]{:S(2)}) collective-permute-start(bf16[1024,512]{1,0:T(8,128)(2,1)} %constant_dynamic-slice_fusion.6), channel_id=1, source_target_pairs={{0,4},{4,0},{8,12},{12,8},{16,20},{20,16},{24,28},{28,24},{1,5},{5... | collective-permute-start | bytes 3145736 | tf_op jit(solution)/shard_map/ppermute | solution.py:156
  307.6 66.6 %collective-permute-start.20 = (bf16[1024,512]{1,0:T(8,128)(2,1)}, bf16[1024,512]{1,0:T(8,128)(2,1)}, u32[]{:S(2)}, u32[]{:S(2)}) collective-permute-start(bf16[1024,512]{1,0:T(8,128)(2,1)} %pad_maximum_fusion.5), channel_id=1, source_target_pairs={{0,4},{4,0},{8,12},{12,8},{16,20},{20,16},{24,28},{28,24},{1,5},{5... | collective-permute-start | bytes 3145736 | tf_op jit(solution)/shard_map/ppermute | solution.py:156
  370.6 6.3 %collective-permute-start.17 = (bf16[1280,512]{0,1:T(8,128)(2,1)}, bf16[1280,512]{0,1:T(8,128)(2,1)}, u32[]{:S(2)}, u32[]{:S(2)}) collective-permute-start(bf16[1280,512]{0,1:T(8,128)(2,1)} %convolution_convert_fusion.2), channel_id=1, source_target_pairs={{0,1},{1,0},{2,3},{3,2},{4,5},{5,4},{6,7},{7,6},{8,9},{9,8},{10,11... | collective-permute-start | bytes 3932168 | tf_op jit(solution)/shard_map/ppermute | solution.py:156
  373.6 5.7 %collective-permute-start.16 = (bf16[1280,512]{0,1:T(8,128)(2,1)}, bf16[1280,512]{0,1:T(8,128)(2,1)}, u32[]{:S(2)}, u32[]{:S(2)}) collective-permute-start(bf16[1280,512]{0,1:T(8,128)(2,1)} %convolution_convert_fusion.3), channel_id=1, source_target_pairs={{0,1},{1,0},{2,3},{3,2},{4,5},{5,4},{6,7},{7,6},{8,9},{9,8},{10,11... | collective-permute-start | bytes 3932168 | tf_op jit(solution)/shard_map/ppermute | solution.py:156
  374.1 25.1 %collective-permute-start.21 = (bf16[1024,512]{1,0:T(8,128)(2,1)S(1)}, bf16[1024,512]{1,0:T(8,128)(2,1)S(1)}, u32[]{:S(2)}, u32[]{:S(2)}) collective-permute-start(bf16[1024,512]{1,0:T(8,128)(2,1)S(1)} %constant_dynamic-slice_fusion), channel_id=1, source_target_pairs={{0,4},{4,0},{8,12},{12,8},{16,20},{20,16},{24,28},{28,24},{1,5},{5... | collective-permute-start | bytes 3145736 | tf_op jit(solution)/shard_map/ppermute | solution.py:156
  400.2 3.1 collective-permute-start.22
  401.2 4.0 collective-permute-start.23
  401.8 30.8 %collective-permute-start.18 = (bf16[1280,512]{0,1:T(8,128)(2,1)S(1)}, bf16[1280,512]{0,1:T(8,128)(2,1)S(1)}, u32[]{:S(2)}, u32[]{:S(2)}) collective-permute-start(bf16[1280,512]{0,1:T(8,128)(2,1)S(1)} %convolution_add_fusion.2), channel_id=1, source_target_pairs={{0,2},{1,3},{2,0},{3,1},{4,6},{5,7},{6,4},{7,5},{8,10},{9,11},{10,... | collective-permute-start | bytes 3932168 | tf_op jit(solution)/shard_map/ppermute | solution.py:156
  406.3 39.7 %collective-permute-start.24 = (bf16[640,1024]{0,1:T(8,128)(2,1)S(1)}, bf16[640,1024]{0,1:T(8,128)(2,1)S(1)}, u32[]{:S(2)}, u32[]{:S(2)}) collective-permute-start(bf16[640,1024]{0,1:T(8,128)(2,1)S(1)} %pad_maximum_fusion.1), channel_id=1, source_target_pairs={{0,8},{4,12},{8,0},{12,4},{16,24},{20,28},{24,16},{28,20},{1,9},{5... | collective-permute-start | bytes 3932168 | tf_op jit(solution)/shard_map/ppermute | solution.py:156
  433.8 25.9 %collective-permute-start.19 = (bf16[640,512]{0,1:T(8,128)(2,1)}, bf16[640,512]{0,1:T(8,128)(2,1)}, u32[]{:S(2)}, u32[]{:S(2)}) collective-permute-start(bf16[640,512]{0,1:T(8,128)(2,1)} %slice.273), channel_id=1, source_target_pairs={{0,8},{4,12},{8,0},{12,4},{16,24},{20,28},{24,16},{28,20},{1,9},{5... | collective-permute-start | bytes 1966088 | tf_op jit(solution)/shard_map/ppermute | solution.py:156
  447.2 16.0 %collective-permute-start.25 = (bf16[640,512]{0,1:T(8,128)(2,1)}, bf16[640,512]{0,1:T(8,128)(2,1)S(1)}, u32[]{:S(2)}, u32[]{:S(2)}) collective-permute-start(bf16[640,512]{0,1:T(8,128)(2,1)} %fusion.30), channel_id=1, source_target_pairs={{0,2},{1,3},{2,0},{3,1},{4,6},{5,7},{6,4},{7,5},{8,10},{9,11},{10,... | collective-permute-start | bytes 1966088 | tf_op jit(solution)/shard_map/ppermute | solution.py:156
  (20 other events, 301.9 us)
Sparse Core Ops, SparseCore 0:
  8.9 43.1 all-gather.4
  53.6 79.9 all-gather.6
  164.1 39.4 all-gather.8
  300.2 64.5 all-gather.10

commit v3 on v1

--- a/solution.py
+++ b/solution.py
@@ -173,8 +173,8 @@
             for side in (parity, 1 - parity)
         ]
 
-    def close_by(parts):
-        return jnp.concatenate([parts[0], paced(parts[1], 2, pair_line, 1)], axis=0)
+    def close_by(parts, *earlier):
+        return jnp.concatenate([parts[0], paced(parts[1], 2, pair_line, 1, *earlier)], axis=0)
 
     def far_off(parts):
         distant = {
@@ -206,7 +206,7 @@
         lax.all_gather(part, "hidden", axis=1, tiled=True) for part in (tokens, peer_tokens)
     ]
 
-    key_close = close_by(key_parts)
+    key_close = close_by(key_parts, value_close)
     query_close = close_by(query_parts)
     query_far = far_off(query_parts)
     out_close = close_by(halves(w_out, 0))

time: 390 us -> 390 us (level)
    unnamed x93 -> x95, local copies, waits for them, and re-layouts: 10.9 us -> 10.9 us
where the time goes in v3:
time: 390 us; the launch traced here: 386 us
  waiting for transfers between devices  174 us (45%)
  starting transfers between devices  62.7 us (16%)
  matrix products  53 us (14%)
  Pallas kernels  28.8 us (7%)
  other arithmetic  27.9 us (7%)
  local copies, waits for them, and re-layouts  25.4 us (7%)
  between operations  14.1 us (4%)
    ppermute x26, waiting for transfers between devices, swap(): return lax.ppermute(value, axis, [(i, i ^ step) for i in range(count)])  163 us
    ppermute x26, starting transfers between devices, swap(): return lax.ppermute(value, axis, [(i, i ^ step) for i in range(count)])  62.4 us
    dot_general x12, matrix products, project(): term = jnp.dot(part, rows, preferred_element_type=jnp.float32)  39.6 us
    pallas_call x1, Pallas kernels, attend(): pl.pallas_call(functools.partial(attention_kernel, width), grid=(groups,...  22.5 us
    dot_general x8, matrix products, block(): return jnp.dot(attended, chosen, preferred_element_type=jnp.float32)  13.4 us
    select_n x1, other arithmetic, bias_tiles(): tiles = jnp.where(buckets == level, table[level][:, None, None], tiles)  12.1 us
    unnamed x95, local copies, waits for them, and re-layouts  10.9 us
    all_gather x2, waiting for transfers between devices, gathered(): lax.all_gather(close, 'batch', axis=0, tiled=True, axis_index_groups=groups)  10.5 us
  transfers between devices with their start and end apart: 30, of which 15 were waited for; matrix products, arithmetic and copies ran while one was open for 24% of the time, Pallas kernels for 7%

profile of v3, /device:TPU:0, one launch (start us, length us, event | category | flops | bytes accessed | tf_op | source)
XLA Modules:
  0.0 386.2 jit_solution(12091260213718738318)
XLA Ops:
  8.7 5.1 %collective-permute-start.2 = (bf16[512,512]{1,0:T(8,128)(2,1)S(1)}, bf16[512,512]{1,0:T(8,128)(2,1)S(1)}, u32[]{:S(2)}, u32[]{:S(2)}) collective-permute-start(bf16[512,512]{1,0:T(8,128)(2,1)S(1)} %get-tuple-element.21), channel_id=1, source_target_pairs={{0,24},{4,28},{8,16},{12,20},{16,8},{20,12},{24,0},{28,4},{1,25},{... | collective-permute-start | bytes 1572872 | tf_op jit(solution)/shard_map/ppermute | solution.py:156
  14.0 12.7 %collective-permute-done.2 = bf16[512,512]{1,0:T(8,128)(2,1)S(1)} collective-permute-done((bf16[512,512]{1,0:T(8,128)(2,1)S(1)}, bf16[512,512]{1,0:T(8,128)(2,1)S(1)}, u32[]{:S(2)}, u32[]{:S(2)}) %collective-permute-start.2) | collective-permute-done | bytes 524320 | tf_op jit(solution)/shard_map/ppermute | solution.py:156
  26.7 10.4 %collective-permute-done.1 = bf16[512,512]{1,0:T(8,128)(2,1)S(1)} collective-permute-done((bf16[512,512]{1,0:T(8,128)(2,1)S(1)}, bf16[512,512]{1,0:T(8,128)(2,1)S(1)}, u32[]{:S(2)}, u32[]{:S(2)}) %collective-permute-start.1) | collective-permute-done | bytes 524320 | tf_op jit(solution)/shard_map/ppermute | solution.py:156
  38.8 29.2 %collective-permute-done.3 = bf16[640,1024]{1,0:T(8,128)(2,1)} collective-permute-done((bf16[640,1024]{1,0:T(8,128)(2,1)S(1)}, bf16[640,1024]{1,0:T(8,128)(2,1)}, u32[]{:S(2)}, u32[]{:S(2)}) %collective-permute-start.3) | collective-permute-done | bytes 1310752 | tf_op jit(solution)/shard_map/ppermute | solution.py:156
  72.7 18.3 %collective-permute-done.4 = bf16[512,512]{1,0:T(8,128)(2,1)S(1)} collective-permute-done((bf16[512,512]{1,0:T(8,128)(2,1)S(1)}, bf16[512,512]{1,0:T(8,128)(2,1)S(1)}, u32[]{:S(2)}, u32[]{:S(2)}) %collective-permute-start.4) | collective-permute-done | bytes 524320 | tf_op jit(solution)/shard_map/ppermute | solution.py:156
  93.3 3.1 broadcast_compare_fusion.26
  102.1 2.6 collective-permute-start.7
  105.9 10.6 %collective-permute-done.5 = bf16[512,512]{1,0:T(8,128)(2,1)S(1)} collective-permute-done((bf16[512,512]{1,0:T(8,128)(2,1)}, bf16[512,512]{1,0:T(8,128)(2,1)S(1)}, u32[]{:S(2)}, u32[]{:S(2)}) %collective-permute-start.5) | collective-permute-done | bytes 524320 | tf_op jit(solution)/shard_map/ppermute | solution.py:156
  122.4 12.1 %select_select_fusion.bias = f32[8,640,128]{2,1,0:T(8,128)} fusion(f32[8]{0:T(128)S(1)} %get-tuple-element.36, f32[8]{0:T(128)S(1)} %get-tuple-element.37, f32[8]{0:T(128)S(1)} %get-tuple-element.38, f32[8]{0:T(128)S(1)} %get-tuple-element.39, f32[8]{0:T(128)S(1)} %get-tuple-element.40, f32[8]{0:T(128)S(1)} %get-tuple-element.41, ...), kind=kLoop, calls=%fused_computation.23 | loop fusion | flops 20971520 | bytes 5243904 | tf_op jit(solution)/shard_map/jit(_where)/select_n | solution.py:35
  134.6 34.4 %collective-permute-done.7 = bf16[512,512]{1,0:T(8,128)(2,1)} collective-permute-done((bf16[512,512]{1,0:T(8,128)(2,1)S(1)}, bf16[512,512]{1,0:T(8,128)(2,1)}, u32[]{:S(2)}, u32[]{:S(2)}) %collective-permute-start.7) | collective-permute-done | bytes 524320 | tf_op jit(solution)/shard_map/ppermute | solution.py:156
  174.2 2.5 copy-done.3
  176.7 2.5 copy-done.4
  179.1 6.4 %shard_map.82 = bf16[1280,4096]{1,0:T(8,128)(2,1)S(1)} custom-call(s32[8]{0:T(128)S(1)} %stack.45.sources, f32[1,4096]{1,0:T(1,128)S(1)} %bitcast.35, bf16[640,4096]{1,0:T(8,128)(2,1)S(1)} %copy-done.3, bf16[640,4096]{1,0:T(8,128)(2,1)S(1)} %copy-done.4), custom_call_target="tpu_custom_call" | custom-call | flops 41943040 | bytes 20971520 | tf_op jit(solution)/shard_map/pallas_call | solution.py:121
  186.8 3.6 fusion.23
  190.4 3.0 fusion.25
  193.4 3.7 fusion.11
  197.1 3.7 fusion.17
  200.9 4.3 %fusion.19 = f32[1280,512]{1,0:T(8,128)} fusion(bf16[1024,512]{1,0:T(8,128)(2,1)} %collective-permute-done.10, bf16[1280,4096]{1,0:T(8,128)(2,1)S(1)} %bitcast.32), kind=kOutput, calls=%fused_computation.35 | convolution fusion | flops 1342177280 | bytes 6291456 | tf_op jit(solution)/shard_map/dot_general | solution.py:236
  205.1 4.4 %fusion.13 = f32[1280,512]{1,0:T(8,128)} fusion(bf16[1024,512]{1,0:T(8,128)(2,1)} %collective-permute-done.11, bf16[1280,4096]{1,0:T(8,128)(2,1)S(1)} %bitcast.32), kind=kOutput, calls=%fused_computation.29 | convolution fusion | flops 1342177280 | bytes 6291456 | tf_op jit(solution)/shard_map/dot_general | solution.py:236
  213.9 6.4 %fusion.6.queries = bf16[1280,512]{1,0:T(8,128)(2,1)S(1)} fusion(f32[1280,512]{1,0:T(8,128)} %fusion.13, f32[1280,512]{1,0:T(8,128)} %fusion.19, f32[1280,512]{1,0:T(8,128)} %fusion.25, bf16[1280,4096]{1,0:T(8,128)(2,1)} %copy-done.2, bf16[512,512]{1,0:T(8,128)(2,1)} %copy-done.21, bf16[512,512]{1,0:T(8,128)(2,1)S(1)} %get-tuple-element.23), kind=kOutput, calls=%fused_computation.13 | convolution fusion | flops 1346895872 | bytes 12845056 | tf_op jit(solution)/shard_map/dot_general | solution.py:236
  220.3 3.9 %fusion.15 = f32[1280,512]{1,0:T(8,128)S(1)} fusion(bf16[1024,512]{1,0:T(8,128)(2,1)} %collective-permute-done.9, bf16[1280,4096]{1,0:T(8,128)(2,1)} %copy-done.2), kind=kOutput, calls=%fused_computation.31 | convolution fusion | flops 1342177280 | bytes 6291456 | tf_op jit(solution)/shard_map/dot_general | solution.py:236
  225.8 5.2 %collective-permute-done.14 = bf16[1024,512]{1,0:T(8,128)(2,1)S(1)} collective-permute-done((bf16[1024,512]{1,0:T(8,128)(2,1)S(1)}, bf16[1024,512]{1,0:T(8,128)(2,1)S(1)}, u32[]{:S(2)}, u32[]{:S(2)}) %collective-permute-start.14) | collective-permute-done | bytes 1048608 | tf_op jit(solution)/shard_map/ppermute | solution.py:156
  234.7 22.5 %shard_map.83 = bf16[1280,512]{1,0:T(8,128)(2,1)S(1)} custom-call(s32[2,1,640]{2,1,0:T(1,128)S(1)} %broadcast_in_dim.413.q_ids, s32[1280,128]{1,0:T(8,128)S(1)} %broadcast_in_dim.415.k_ids, f32[8,640,128]{2,1,0:T(8,128)S(1)} %copy-done.5, bf16[1280,512]{1,0:T(8,128)(2,1)S(1)} %fusion.6.queries, bf16[1280,512]{1,0:T(8,128)(2,1)S(1)} %fusion.7.keys, ...), custom_call_target="tpu_custom_call" | custom-call | flops 3355443200 | bytes 10485760 | tf_op jit(solution)/shard_map/pallas_call | solution.py:81
  257.2 10.5 %all-gather.11.cloned.1.call-done = bf16[2048,512]{1,0:T(8,128)(2,1)} async-done(((bf16[1024,512]{1,0:T(8,128)(2,1)}), bf16[2048,512]{1,0:T(8,128)(2,1)}) %all-gather.11.cloned.1.call-update) | async-done | bytes 2097168 | tf_op jit(solution)/shard_map/all_gather | solution.py:189
  273.5 3.0 convolution_convert_fusion.3
  282.2 2.4 convolution_add_fusion.3
  284.6 17.5 %collective-permute-done.21 = bf16[1024,512]{1,0:T(8,128)(2,1)S(1)} collective-permute-done((bf16[1024,512]{1,0:T(8,128)(2,1)S(1)}, bf16[1024,512]{1,0:T(8,128)(2,1)S(1)}, u32[]{:S(2)}, u32[]{:S(2)}) %collective-permute-start.21) | collective-permute-done | bytes 1048608 | tf_op jit(solution)/shard_map/ppermute | solution.py:156
  309.2 17.4 %collective-permute-start.24 = (bf16[640,1024]{0,1:T(8,128)(2,1)S(1)}, bf16[640,1024]{0,1:T(8,128)(2,1)S(1)}, u32[]{:S(2)}, u32[]{:S(2)}) collective-permute-start(bf16[640,1024]{0,1:T(8,128)(2,1)S(1)} %pad_maximum_fusion.1), channel_id=1, source_target_pairs={{0,8},{4,12},{8,0},{12,4},{16,24},{20,28},{24,16},{28,20},{1,9},{5... | collective-permute-start | bytes 3932168 | tf_op jit(solution)/shard_map/ppermute | solution.py:156
  326.6 8.8 %collective-permute-done.18 = bf16[1280,512]{0,1:T(8,128)(2,1)S(1)} collective-permute-done((bf16[1280,512]{0,1:T(8,128)(2,1)S(1)}, bf16[1280,512]{0,1:T(8,128)(2,1)S(1)}, u32[]{:S(2)}, u32[]{:S(2)}) %collective-permute-start.18) | collective-permute-done | bytes 1310752 | tf_op jit(solution)/shard_map/ppermute | solution.py:156
  336.6 17.3 %collective-permute-start.19 = (bf16[640,512]{0,1:T(8,128)(2,1)}, bf16[640,512]{0,1:T(8,128)(2,1)}, u32[]{:S(2)}, u32[]{:S(2)}) collective-permute-start(bf16[640,512]{0,1:T(8,128)(2,1)} %slice.273), channel_id=1, source_target_pairs={{0,8},{4,12},{8,0},{12,4},{16,24},{20,28},{24,16},{28,20},{1,9},{5... | collective-permute-start | bytes 1966088 | tf_op jit(solution)/shard_map/ppermute | solution.py:156
  358.9 10.9 %collective-permute-done.19 = bf16[640,512]{0,1:T(8,128)(2,1)} collective-permute-done((bf16[640,512]{0,1:T(8,128)(2,1)}, bf16[640,512]{0,1:T(8,128)(2,1)}, u32[]{:S(2)}, u32[]{:S(2)}) %collective-permute-start.19) | collective-permute-done | bytes 655392 | tf_op jit(solution)/shard_map/ppermute | solution.py:156
  375.9 3.6 add_convert_fusion
  (188 shorter events, 70.4 us)
Async XLA Ops:
  6.5 89.8 %copy-start = (f32[32,16]{0,1:T(8,128)S(1)}, f32[32,16]{0,1:T(8,128)}, u32[]{:S(2)}) copy-start(f32[32,16]{0,1:T(8,128)} %param.10) | copy-start | bytes 6148
  6.5 114.6 %all-gather.5.cloned.1.call-start = ((), (), s32[]{:S(2)}) async-start(), calls=%async_computation | async-start | bytes 6553600 | tf_op jit(solution)/shard_map/all_gather | solution.py:206
  7.3 166.9 %all-gather.7.cloned.1.call-start = ((), (), s32[]{:S(2)}) async-start(), calls=%async_computation.1 | async-start | bytes 6553600 | tf_op jit(solution)/shard_map/all_gather | solution.py:206
  8.7 82.3 %copy-start.11 = (bf16[512,512]{1,0:T(8,128)(2,1)}, bf16[512,512]{1,0:T(8,128)(2,1)S(1)}, u32[]{:S(2)}) copy-start(bf16[512,512]{1,0:T(8,128)(2,1)S(1)} %get-tuple-element.72) | copy-start | bytes 1572868
  8.7 18.0 %collective-permute-start.2 = (bf16[512,512]{1,0:T(8,128)(2,1)S(1)}, bf16[512,512]{1,0:T(8,128)(2,1)S(1)}, u32[]{:S(2)}, u32[]{:S(2)}) collective-permute-start(bf16[512,512]{1,0:T(8,128)(2,1)S(1)} %get-tuple-element.21), channel_id=1, source_target_pairs={{0,24},{4,28},{8,16},{12,20},{16,8},{20,12},{24,0},{28,4},{1,25},{... | collective-permute-start | bytes 1572872 | tf_op jit(solution)/shard_map/ppermute | solution.py:156
  13.9 23.1 %collective-permute-start.1 = (bf16[512,512]{1,0:T(8,128)(2,1)S(1)}, bf16[512,512]{1,0:T(8,128)(2,1)S(1)}, u32[]{:S(2)}, u32[]{:S(2)}) collective-permute-start(bf16[512,512]{1,0:T(8,128)(2,1)S(1)} %get-tuple-element.70), channel_id=1, source_target_pairs={{0,8},{4,12},{8,0},{12,4},{16,24},{20,28},{24,16},{28,20},{1,9},{5... | collective-permute-start | bytes 1572872 | tf_op jit(solution)/shard_map/ppermute | solution.py:156
  37.1 30.9 %collective-permute-start.3 = (bf16[640,1024]{1,0:T(8,128)(2,1)S(1)}, bf16[640,1024]{1,0:T(8,128)(2,1)}, u32[]{:S(2)}, u32[]{:S(2)}) collective-permute-start(bf16[640,1024]{1,0:T(8,128)(2,1)S(1)} %copy-done.10), channel_id=1, source_target_pairs={{0,8},{4,12},{8,0},{12,4},{16,24},{20,28},{24,16},{28,20},{1,9},{5... | collective-permute-start | bytes 3932168 | tf_op jit(solution)/shard_map/ppermute | solution.py:156
  68.0 143.3 %all-gather.9.cloned.1.call-start = ((), (), s32[]{:S(2)}) async-start(), calls=%async_computation.2 | async-start | bytes 3145728 | tf_op jit(solution)/shard_map/all_gather | solution.py:189
  69.2 21.8 %collective-permute-start.4 = (bf16[512,512]{1,0:T(8,128)(2,1)S(1)}, bf16[512,512]{1,0:T(8,128)(2,1)S(1)}, u32[]{:S(2)}, u32[]{:S(2)}) collective-permute-start(bf16[512,512]{1,0:T(8,128)(2,1)S(1)} %copy-done.27), channel_id=1, source_target_pairs={{0,8},{4,12},{8,0},{12,4},{16,24},{20,28},{24,16},{28,20},{1,9},{5... | collective-permute-start | bytes 1572872 | tf_op jit(solution)/shard_map/ppermute | solution.py:156
  69.9 32.2 %collective-permute-start.6 = (bf16[512,512]{1,0:T(8,128)(2,1)S(1)}, bf16[512,512]{1,0:T(8,128)(2,1)}, u32[]{:S(2)}, u32[]{:S(2)}) collective-permute-start(bf16[512,512]{1,0:T(8,128)(2,1)S(1)} %get-tuple-element.72), channel_id=1, source_target_pairs={{0,16},{4,20},{8,24},{12,28},{16,0},{20,4},{24,8},{28,12},{1,17},{... | collective-permute-start | bytes 1572872 | tf_op jit(solution)/shard_map/ppermute | solution.py:156
  70.6 50.8 %collective-permute-start = (s32[1,640]{1,0:T(1,128)S(1)}, s32[1,640]{1,0:T(1,128)S(1)}, u32[]{:S(2)}, u32[]{:S(2)}) collective-permute-start(s32[1,640]{1,0:T(1,128)S(1)} %copy-done.34), channel_id=1, source_target_pairs={{0,8},{4,12},{8,0},{12,4},{16,24},{20,28},{24,16},{28,20},{1,9},{5... | collective-permute-start | bytes 7688 | tf_op jit(solution)/shard_map/ppermute | solution.py:156
  71.2 48.8 %collective-permute-start.9 = (bf16[1024,512]{1,0:T(8,128)(2,1)}, bf16[1024,512]{1,0:T(8,128)(2,1)}, u32[]{:S(2)}, u32[]{:S(2)}) collective-permute-start(bf16[1024,512]{1,0:T(8,128)(2,1)} %pad_maximum_fusion.2), channel_id=1, source_target_pairs={{0,4},{4,0},{8,12},{12,8},{16,20},{20,16},{24,28},{28,24},{1,5},{5... | collective-permute-start | bytes 3145736 | tf_op jit(solution)/shard_map/ppermute | solution.py:156
  92.1 29.0 %collective-permute-start.12 = (bf16[1024,512]{1,0:T(8,128)(2,1)}, bf16[1024,512]{1,0:T(8,128)(2,1)}, u32[]{:S(2)}, u32[]{:S(2)}) collective-permute-start(bf16[1024,512]{1,0:T(8,128)(2,1)} %pad_maximum_fusion.4), channel_id=1, source_target_pairs={{0,4},{4,0},{8,12},{12,8},{16,20},{20,16},{24,28},{28,24},{1,5},{5... | collective-permute-start | bytes 3145736 | tf_op jit(solution)/shard_map/ppermute | solution.py:156
  98.5 18.0 %collective-permute-start.5 = (bf16[512,512]{1,0:T(8,128)(2,1)}, bf16[512,512]{1,0:T(8,128)(2,1)S(1)}, u32[]{:S(2)}, u32[]{:S(2)}) collective-permute-start(bf16[512,512]{1,0:T(8,128)(2,1)} %get-tuple-element.22), channel_id=1, source_target_pairs={{0,8},{4,12},{8,0},{12,4},{16,24},{20,28},{24,16},{28,20},{1,9},{5... | collective-permute-start | bytes 1572872 | tf_op jit(solution)/shard_map/ppermute | solution.py:156
  102.1 66.9 %collective-permute-start.7 = (bf16[512,512]{1,0:T(8,128)(2,1)S(1)}, bf16[512,512]{1,0:T(8,128)(2,1)}, u32[]{:S(2)}, u32[]{:S(2)}) collective-permute-start(bf16[512,512]{1,0:T(8,128)(2,1)S(1)} %get-tuple-element.23), channel_id=1, source_target_pairs={{0,16},{4,20},{8,24},{12,28},{16,0},{20,4},{24,8},{28,12},{1,17},{... | collective-permute-start | bytes 1572872 | tf_op jit(solution)/shard_map/ppermute | solution.py:156
  116.5 53.5 %collective-permute-start.8 = (bf16[512,512]{1,0:T(8,128)(2,1)}, bf16[512,512]{1,0:T(8,128)(2,1)}, u32[]{:S(2)}, u32[]{:S(2)}) collective-permute-start(bf16[512,512]{1,0:T(8,128)(2,1)} %get-tuple-element.22), channel_id=1, source_target_pairs={{0,24},{4,28},{8,16},{12,20},{16,8},{20,12},{24,0},{28,4},{1,25},{... | collective-permute-start | bytes 1572872 | tf_op jit(solution)/shard_map/ppermute | solution.py:156
  120.0 53.3 %collective-permute-start.10 = (bf16[1024,512]{1,0:T(8,128)(2,1)}, bf16[1024,512]{1,0:T(8,128)(2,1)}, u32[]{:S(2)}, u32[]{:S(2)}) collective-permute-start(bf16[1024,512]{1,0:T(8,128)(2,1)} %pad_maximum_fusion.3), channel_id=1, source_target_pairs={{0,4},{4,0},{8,12},{12,8},{16,20},{20,16},{24,28},{28,24},{1,5},{5... | collective-permute-start | bytes 3145736 | tf_op jit(solution)/shard_map/ppermute | solution.py:156
  121.1 50.1 %collective-permute-start.15 = (bf16[512,512]{1,0:T(8,128)(2,1)}, bf16[512,512]{1,0:T(8,128)(2,1)S(1)}, u32[]{:S(2)}, u32[]{:S(2)}) collective-permute-start(bf16[512,512]{1,0:T(8,128)(2,1)} %get-tuple-element.30), channel_id=1, source_target_pairs={{0,8},{4,12},{8,0},{12,4},{16,24},{20,28},{24,16},{28,20},{1,9},{5... | collective-permute-start | bytes 1572872 | tf_op jit(solution)/shard_map/ppermute | solution.py:156
  121.1 146.6 %all-gather.11.cloned.1.call-start = ((), (), s32[]{:S(2)}) async-start(), calls=%async_computation.3 | async-start | bytes 3145728 | tf_op jit(solution)/shard_map/all_gather | solution.py:189
  121.4 64.2 %collective-permute-start.13 = (bf16[1024,512]{1,0:T(8,128)(2,1)}, bf16[1024,512]{1,0:T(8,128)(2,1)}, u32[]{:S(2)}, u32[]{:S(2)}) collective-permute-start(bf16[1024,512]{1,0:T(8,128)(2,1)} %copy-done.32), channel_id=1, source_target_pairs={{0,4},{4,0},{8,12},{12,8},{16,20},{20,16},{24,28},{28,24},{1,5},{5... | collective-permute-start | bytes 3145736 | tf_op jit(solution)/shard_map/ppermute | solution.py:156
  173.3 31.8 %collective-permute-start.11 = (bf16[1024,512]{1,0:T(8,128)(2,1)}, bf16[1024,512]{1,0:T(8,128)(2,1)}, u32[]{:S(2)}, u32[]{:S(2)}) collective-permute-start(bf16[1024,512]{1,0:T(8,128)(2,1)} %copy-done.30), channel_id=1, source_target_pairs={{0,4},{4,0},{8,12},{12,8},{16,20},{20,16},{24,28},{28,24},{1,5},{5... | collective-permute-start | bytes 3145736 | tf_op jit(solution)/shard_map/ppermute | solution.py:156
  185.5 91.5 %collective-permute-start.20 = (bf16[1024,512]{1,0:T(8,128)(2,1)}, bf16[1024,512]{1,0:T(8,128)(2,1)}, u32[]{:S(2)}, u32[]{:S(2)}) collective-permute-start(bf16[1024,512]{1,0:T(8,128)(2,1)} %pad_maximum_fusion.5), channel_id=1, source_target_pairs={{0,4},{4,0},{8,12},{12,8},{16,20},{20,16},{24,28},{28,24},{1,5},{5... | collective-permute-start | bytes 3145736 | tf_op jit(solution)/shard_map/ppermute | solution.py:156
  212.6 18.3 %collective-permute-start.14 = (bf16[1024,512]{1,0:T(8,128)(2,1)S(1)}, bf16[1024,512]{1,0:T(8,128)(2,1)S(1)}, u32[]{:S(2)}, u32[]{:S(2)}) collective-permute-start(bf16[1024,512]{1,0:T(8,128)(2,1)S(1)} %constant_dynamic-slice_fusion.3), channel_id=1, source_target_pairs={{0,4},{4,0},{8,12},{12,8},{16,20},{20,16},{24,28},{28,24},{1,5},{5... | collective-permute-start | bytes 3145736 | tf_op jit(solution)/shard_map/ppermute | solution.py:156
  273.5 6.3 %collective-permute-start.17 = (bf16[1280,512]{0,1:T(8,128)(2,1)}, bf16[1280,512]{0,1:T(8,128)(2,1)}, u32[]{:S(2)}, u32[]{:S(2)}) collective-permute-start(bf16[1280,512]{0,1:T(8,128)(2,1)} %convolution_convert_fusion.2), channel_id=1, source_target_pairs={{0,1},{1,0},{2,3},{3,2},{4,5},{5,4},{6,7},{7,6},{8,9},{9,8},{10,11... | collective-permute-start | bytes 3932168 | tf_op jit(solution)/shard_map/ppermute | solution.py:156
  276.5 5.7 %collective-permute-start.16 = (bf16[1280,512]{0,1:T(8,128)(2,1)}, bf16[1280,512]{0,1:T(8,128)(2,1)}, u32[]{:S(2)}, u32[]{:S(2)}) collective-permute-start(bf16[1280,512]{0,1:T(8,128)(2,1)} %convolution_convert_fusion.3), channel_id=1, source_target_pairs={{0,1},{1,0},{2,3},{3,2},{4,5},{5,4},{6,7},{7,6},{8,9},{9,8},{10,11... | collective-permute-start | bytes 3932168 | tf_op jit(solution)/shard_map/ppermute | solution.py:156
  277.0 25.1 %collective-permute-start.21 = (bf16[1024,512]{1,0:T(8,128)(2,1)S(1)}, bf16[1024,512]{1,0:T(8,128)(2,1)S(1)}, u32[]{:S(2)}, u32[]{:S(2)}) collective-permute-start(bf16[1024,512]{1,0:T(8,128)(2,1)S(1)} %constant_dynamic-slice_fusion), channel_id=1, source_target_pairs={{0,4},{4,0},{8,12},{12,8},{16,20},{20,16},{24,28},{28,24},{1,5},{5... | collective-permute-start | bytes 3145736 | tf_op jit(solution)/shard_map/ppermute | solution.py:156
  303.1 3.1 collective-permute-start.22
  304.0 4.0 %collective-permute-start.23 = (bf16[1280,512]{0,1:T(8,128)(2,1)S(1)}, bf16[1280,512]{0,1:T(8,128)(2,1)S(1)}, u32[]{:S(2)}, u32[]{:S(2)}) collective-permute-start(bf16[1280,512]{0,1:T(8,128)(2,1)S(1)} %convolution_convert_fusion), channel_id=1, source_target_pairs={{0,1},{1,0},{2,3},{3,2},{4,5},{5,4},{6,7},{7,6},{8,9},{9,8},{10,11... | collective-permute-start | bytes 3932168 | tf_op jit(solution)/shard_map/ppermute | solution.py:156
  304.6 30.8 %collective-permute-start.18 = (bf16[1280,512]{0,1:T(8,128)(2,1)S(1)}, bf16[1280,512]{0,1:T(8,128)(2,1)S(1)}, u32[]{:S(2)}, u32[]{:S(2)}) collective-permute-start(bf16[1280,512]{0,1:T(8,128)(2,1)S(1)} %convolution_add_fusion.2), channel_id=1, source_target_pairs={{0,2},{1,3},{2,0},{3,1},{4,6},{5,7},{6,4},{7,5},{8,10},{9,11},{10,... | collective-permute-start | bytes 3932168 | tf_op jit(solution)/shard_map/ppermute | solution.py:156
  309.2 47.0 %collective-permute-start.24 = (bf16[640,1024]{0,1:T(8,128)(2,1)S(1)}, bf16[640,1024]{0,1:T(8,128)(2,1)S(1)}, u32[]{:S(2)}, u32[]{:S(2)}) collective-permute-start(bf16[640,1024]{0,1:T(8,128)(2,1)S(1)} %pad_maximum_fusion.1), channel_id=1, source_target_pairs={{0,8},{4,12},{8,0},{12,4},{16,24},{20,28},{24,16},{28,20},{1,9},{5... | collective-permute-start | bytes 3932168 | tf_op jit(solution)/shard_map/ppermute | solution.py:156
  336.6 33.2 %collective-permute-start.19 = (bf16[640,512]{0,1:T(8,128)(2,1)}, bf16[640,512]{0,1:T(8,128)(2,1)}, u32[]{:S(2)}, u32[]{:S(2)}) collective-permute-start(bf16[640,512]{0,1:T(8,128)(2,1)} %slice.273), channel_id=1, source_target_pairs={{0,8},{4,12},{8,0},{12,4},{16,24},{20,28},{24,16},{28,20},{1,9},{5... | collective-permute-start | bytes 1966088 | tf_op jit(solution)/shard_map/ppermute | solution.py:156
  357.4 16.0 %collective-permute-start.25 = (bf16[640,512]{0,1:T(8,128)(2,1)}, bf16[640,512]{0,1:T(8,128)(2,1)S(1)}, u32[]{:S(2)}, u32[]{:S(2)}) collective-permute-start(bf16[640,512]{0,1:T(8,128)(2,1)} %fusion.30), channel_id=1, source_target_pairs={{0,2},{1,3},{2,0},{3,1},{4,6},{5,7},{6,4},{7,5},{8,10},{9,11},{10,... | collective-permute-start | bytes 1966088 | tf_op jit(solution)/shard_map/ppermute | solution.py:156
  (44 other events, 670.7 us)
Sparse Core Ops, SparseCore 0:
  8.9 43.1 all-gather.4
  68.2 38.7 all-gather.6
  121.3 73.4 all-gather.8
  196.2 71.4 all-gather.10
